TPU v7x, 256 devices: a whole 4x4x8 slice. The times are simulated.
256 devices in a mesh: frames: 16 (over z_lo, x), verts: 16 (over y, z_hi, core).
Axes of the slice: x: 4, y: 4, z: 8 (z_hi: 2, z_lo: 4; z = z_hi * 4 + z_lo), core: 2. Of those that a mesh axis runs over, the one named last changes fastest.
Arguments:
- observed: bfloat16 [16384, 65536], P('frames', 'verts'), may hold values from -16 to 16
- mask: int32 [16384, 512], P('frames', 'verts'), may hold values 0 or 1
- basis: bfloat16 [65536, 256], P('verts'), may hold values from -6 to 6
- coeffs: float32 [16384, 256], P(('frames', 'verts')), may hold values from -6 to 6
- lag_set: int32 [8], replicated, may hold values from 1 to 32, as said below
- ar_weight: float32 [8, 256], replicated, may hold values from -0.6 to 0.6
Outputs:
- new_coeffs: float32 [16384, 256], P(('frames', 'verts'))
- new_basis: bfloat16 [65536, 256], P('verts')
Inputs may be any that keep to these rules, and one draw needn't show every extreme that they name: `lag_set`: distinct lags; both 1 and 32 are among them.
All inputs are finite; a program needn't handle non-finite values. No bound on the sum of `mask` on one device may be relied on, other than what follows from the above.
Results may differ from a plain program's by a relative error of at most 0.0038.
Values may be sent and summed in bfloat16 or wider, within the bound.
A program may use at most 128 MiB of HBM per device.

v0:
```python
import jax
import jax.numpy as jnp
from jax import lax
from jax.sharding import PartitionSpec as P

R = 256
NLAG = 8
LAGMAX = 32
GRP = 128


def shortened(shard):

    def short(part):
        return part.astype(jnp.bfloat16) if part.dtype == jnp.float32 else part

    return jax.tree.map(short, shard)


def shifted(shard, axis, by):
    peers = lax.axis_size(axis)
    pairs = [(i, i + by) for i in range(peers) if 0 <= i + by < peers]
    return lax.ppermute(shard, axis, pairs)


def residual_rows(obs_rows, mask_rows, coeff_low, basis):
    prod = lax.dot_general(
        coeff_low, basis, (((1,), (1,)), ((), ())), preferred_element_type=jnp.float32
    ) * R ** (-0.5)
    diff = prod - obs_rows.astype(jnp.float32)
    rows = diff.shape[0]
    shaped = diff.reshape(rows, mask_rows.shape[1], GRP) * mask_rows.astype(jnp.float32)[:, :, None]
    return shaped.reshape(rows, -1).astype(jnp.bfloat16)


def prior_local(coeff, lag_set, ar_weight):
    rows = coeff.shape[0]
    base = lax.axis_index(("frames", "verts")) * rows
    lower = shifted(shortened(coeff[rows - LAGMAX :]), ("frames", "verts"), 1)
    front = jnp.concatenate([lower, coeff], axis=0)
    resid = coeff
    for index in range(NLAG):
        start = LAGMAX - lag_set[index]
        resid = resid - ar_weight[index] * lax.dynamic_slice_in_dim(front, start, rows, 0)
    frame = base + jnp.arange(rows, dtype=jnp.int32)
    resid = jnp.where((frame >= LAGMAX)[:, None], resid, jnp.zeros_like(resid))
    upper = shifted(shortened(resid[:LAGMAX]), ("frames", "verts"), -1)
    back = jnp.concatenate([resid, upper], axis=0)
    grad = resid
    for index in range(NLAG):
        start = lag_set[index]
        grad = grad - ar_weight[index] * lax.dynamic_slice_in_dim(back, start, rows, 0)
    return grad


def shards(observed, mask, basis, coeffs, lag_set, ar_weight):
    frame_rows = observed.shape[0]
    verts_size = lax.axis_size("verts")
    frames_size = lax.axis_size("frames")
    joined_size = verts_size * frames_size
    owned = coeffs.shape[0]

    def error_rows(piece):
        return residual_rows(observed, mask, piece, basis)

    err = error_rows(lax.all_gather(coeffs.astype(jnp.bfloat16), "verts", axis=0, tiled=True))
    data_grad = lax.psum_scatter(
        jnp.dot(err, basis, preferred_element_type=jnp.float32) * R ** (-0.5),
        "verts",
        scatter_dimension=0,
        tiled=True,
    )
    scale_nv = (observed.shape[1] * verts_size) ** (-0.5)
    total_entries = owned * joined_size * R
    coeff = coeffs
    for step in range(2):
        grad = data_grad * scale_nv + prior_local(coeff, lag_set, ar_weight)
        squares = lax.psum(jnp.sum(grad * grad), ("frames", "verts"))
        coeff = coeff - 0.3 * grad / jnp.sqrt(squares / total_entries + 1e-06)
    piece = lax.all_gather(coeff.astype(jnp.bfloat16), "verts", axis=0, tiled=True)
    err_next = error_rows(piece)
    partial_value = lax.dot_general(
        err_next, piece, (((0,), (0,)), ((), ())), preferred_element_type=jnp.float32
    )
    step_scale = 2.0 / jnp.sqrt(jnp.float32(frame_rows * frames_size))
    basis_grad = lax.psum(partial_value, "frames") * R ** (-0.5)
    new_basis = (basis.astype(jnp.float32) - step_scale * basis_grad).astype(jnp.bfloat16)
    return (coeff, new_basis)


def solution(mesh):
    placed = (
        P("frames", "verts"),
        P("frames", "verts"),
        P("verts", None),
        P(("frames", "verts"), None),
        P(),
        P(),
    )
    return jax.shard_map(
        shards,
        mesh=mesh,
        in_specs=placed,
        out_specs=(P(("frames", "verts"), None), P("verts", None)),
        check_vma=False,
    )
```

profile of v0, /device:TPU:16, one launch (start us, length us, event | category | flops | bytes accessed | tf_op | source)
XLA Modules:
  0.0 566.6 jit_solution(11757433026159677631)
XLA Ops:
  7.2 0.0 reduce-scatter.2.cloned.1.call-start
  7.2 0.8 convert_element_type.42
  8.1 0.9 convert_element_type.44
  9.0 0.2 copy.8
  9.2 33.7 %all_gather.6 = bf16[1024,256]{1,0:T(8,128)(2,1)S(1)} all-gather(bf16[64,256]{1,0:T(8,128)(2,1)S(1)} %convert_element_type.42), channel_id=1, replica_groups=mesh['frames'=16,'verts'=16] {'verts'}, dimensions={0}, use_global_device_ids=true | all-gather | bytes 557056 | tf_op jit(solution)/shard_map/all_gather | solution.py:66
  42.8 0.0 copy-start
  42.8 11.1 %mul.133 = f32[1024,32,128]{2,1,0:T(8,128)} broadcast(f32[1024,32]{1,0:T(8,128)S(1)} %copy.8), dimensions={0,1} | broadcast | bytes 16908288 | tf_op jit(solution)/shard_map/mul | solution.py:32
  54.0 0.0 copy-done
  54.0 0.0 copy-start.2
  54.0 0.0 copy-start.3
  54.0 0.0 copy-start.1
  54.0 19.8 %fusion.5 = f32[1024,256]{1,0:T(8,128)} fusion(bf16[4096,256]{1,0:T(8,128)(2,1)S(1)} %copy-done, bf16[1024,4096]{1,0:T(8,128)(2,1)} %param.6, f32[128,8,32,128]{3,2,1,0:T(8,128)} %bitcast.31, bf16[1024,256]{1,0:T(8,128)(2,1)S(1)} %all_gather.6), kind=kOutput, calls=%fused_computation.8 | convolution fusion | flops 4316200960 | bytes 28835840 | tf_op jit(solution)/shard_map/dot_general | solution.py:68
  73.8 0.0 reduce-scatter.2.cloned.1.call-update
  73.9 0.0 all-reduce.2.cloned.1.call-start
  73.9 2.3 collective-permute-start
  76.2 0.0 copy-done.2
  76.2 0.7 fusion.111
  76.9 0.0 copy-done.3
  86.9 0.0 collective-permute-done
  87.0 0.0 copy-done.1
  87.0 0.3 fusion.84
  87.2 8.3 %collective-permute-start.1 = (bf16[32,256]{1,0:T(8,128)(2,1)S(1)}, bf16[32,256]{1,0:T(8,128)(2,1)S(1)}, u32[]{:S(2)}, u32[]{:S(2)}) collective-permute-start(bf16[32,256]{1,0:T(8,128)(2,1)S(1)} %slice.141), channel_id=1, source_target_pairs={{1,0},{2,1},{3,2},{4,3},{5,4},{6,5},{7,6},{8,7},{9,8},{10,9},{11,1... | collective-permute-start | bytes 49160 | tf_op jit(solution)/shard_map/ppermute | solution.py:23
  110.6 0.0 collective-permute-done.1
  110.6 41.6 %reduce-scatter.2.cloned.1.call-done = f32[64,256]{1,0:T(8,128)} async-done(((f32[1024,256]{1,0:T(8,128)}), f32[64,256]{1,0:T(8,128)}) %reduce-scatter.2.cloned.1.call-update) | async-done | bytes 65552 | tf_op jit(solution)/shard_map/reduce_scatter | solution.py:67
  152.2 1.8 multiply_reduce_fusion.1
  154.0 73.7 %psum.21 = f32[]{:T(128)} all-reduce(f32[]{:T(128)} %get-tuple-element.6), channel_id=1, replica_groups=mesh['frames'=16,'verts'=16] {'frames','verts'}, use_global_device_ids=true, to_apply=%region_2.3 | all-reduce | flops 1 | bytes 8 | tf_op jit(solution)/shard_map/psum | solution.py:78
  228.4 1.9 collective-permute-start.2
  230.3 7.9 %collective-permute-done.2 = bf16[32,256]{1,0:T(8,128)(2,1)S(1)} collective-permute-done((bf16[32,256]{1,0:T(8,128)(2,1)S(1)}, bf16[32,256]{1,0:T(8,128)(2,1)S(1)}, u32[]{:S(2)}, u32[]{:S(2)}) %collective-permute-start.2) | collective-permute-done | bytes 16416 | tf_op jit(solution)/shard_map/ppermute | solution.py:23
  238.3 0.2 fusion.34
  238.5 1.9 collective-permute-start.3
  240.5 1.4 collective-permute-done.3
  241.9 1.8 multiply_reduce_fusion
  243.7 79.8 %psum.22 = f32[]{:T(128)} all-reduce(f32[]{:T(128)} %get-tuple-element.4), channel_id=1, replica_groups=mesh['frames'=16,'verts'=16] {'frames','verts'}, use_global_device_ids=true, to_apply=%region_4.5 | all-reduce | flops 1 | bytes 8 | tf_op jit(solution)/shard_map/psum | solution.py:78
  324.2 0.6 fusion.107
  324.8 30.7 %all_gather.7 = bf16[1024,256]{1,0:T(8,128)(2,1)S(1)} all-gather(bf16[64,256]{1,0:T(8,128)(2,1)S(1)} %get-tuple-element.2), channel_id=1, replica_groups=mesh['frames'=16,'verts'=16] {'verts'}, dimensions={0}, use_global_device_ids=true | all-gather | bytes 557056 | tf_op jit(solution)/shard_map/all_gather | solution.py:80
  355.5 19.0 %fusion.3 = bf16[1024,4096]{1,0:T(8,128)(2,1)S(1)} fusion(bf16[1024,4096]{1,0:T(8,128)(2,1)} %param.6, f32[128,8,32,128]{3,2,1,0:T(8,128)} %bitcast.32, bf16[1024,256]{1,0:T(8,128)(2,1)S(1)} %all_gather.7, bf16[4096,256]{1,0:T(8,128)(2,1)} %param.8), kind=kOutput, calls=%fused_computation.5 | convolution fusion | flops 2168455168 | bytes 36175872 | tf_op jit(solution)/shard_map/dot_general | solution.py:27
  374.5 4.6 fusion.112
  379.1 0.0 all-reduce.2.cloned.1.call-update
  379.1 176.0 %all-reduce.2.cloned.1.call-done = f32[4096,256]{1,0:T(8,128)} async-done(((f32[4096,256]{1,0:T(8,128)}), f32[4096,256]{1,0:T(8,128)}) %all-reduce.2.cloned.1.call-update) | async-done | bytes 4194320 | tf_op jit(solution)/shard_map/psum | solution.py:86
  555.1 4.7 subtract_convert_fusion
  (11 shorter events, 0.1 us)
Async XLA Ops:
  7.2 145.0 %reduce-scatter.2.cloned.1.call-start = ((), (), s32[]{:S(2)}) async-start(), calls=%async_computation.1 | async-start | bytes 1114112 | tf_op jit(solution)/shard_map/reduce_scatter | solution.py:67
  42.8 11.1 %copy-start = (bf16[4096,256]{1,0:T(8,128)(2,1)S(1)}, bf16[4096,256]{1,0:T(8,128)(2,1)}, u32[]{:S(2)}) copy-start(bf16[4096,256]{1,0:T(8,128)(2,1)} %param.8) | copy-start | bytes 6291460
  54.0 22.2 %copy-start.2 = (s32[8]{0:T(128)S(1)}, s32[8]{0:T(128)}, u32[]{:S(2)}) copy-start(s32[8]{0:T(128)} %param.10) | copy-start | bytes 100
  54.0 22.9 %copy-start.3 = (f32[8,256]{1,0:T(8,128)S(1)}, f32[8,256]{1,0:T(8,128)}, u32[]{:S(2)}) copy-start(f32[8,256]{1,0:T(8,128)} %param.11) | copy-start | bytes 24580
  54.0 33.0 %copy-start.1 = (f32[64,256]{1,0:T(8,128)S(1)}, f32[64,256]{1,0:T(8,128)}, u32[]{:S(2)}) copy-start(f32[64,256]{1,0:T(8,128)} %param.9) | copy-start | bytes 196612
  73.9 481.3 %all-reduce.2.cloned.1.call-start = ((), (), s32[]{:S(2)}) async-start(), calls=%async_computation.2 | async-start | bytes 8388608 | tf_op jit(solution)/shard_map/psum | solution.py:86
  73.9 13.0 %collective-permute-start = (bf16[32,256]{1,0:T(8,128)(2,1)S(1)}, bf16[32,256]{1,0:T(8,128)(2,1)S(1)}, u32[]{:S(2)}, u32[]{:S(2)}) collective-permute-start(bf16[32,256]{1,0:T(8,128)(2,1)S(1)} %slice.64), channel_id=1, source_target_pairs={{0,1},{1,2},{2,3},{3,4},{4,5},{5,6},{6,7},{7,8},{8,9},{9,10},{10,1... | collective-permute-start | bytes 49160 | tf_op jit(solution)/shard_map/ppermute | solution.py:23
  87.2 23.3 %collective-permute-start.1 = (bf16[32,256]{1,0:T(8,128)(2,1)S(1)}, bf16[32,256]{1,0:T(8,128)(2,1)S(1)}, u32[]{:S(2)}, u32[]{:S(2)}) collective-permute-start(bf16[32,256]{1,0:T(8,128)(2,1)S(1)} %slice.141), channel_id=1, source_target_pairs={{1,0},{2,1},{3,2},{4,3},{5,4},{6,5},{7,6},{8,7},{9,8},{10,9},{11,1... | collective-permute-start | bytes 49160 | tf_op jit(solution)/shard_map/ppermute | solution.py:23
  228.4 9.9 %collective-permute-start.2 = (bf16[32,256]{1,0:T(8,128)(2,1)S(1)}, bf16[32,256]{1,0:T(8,128)(2,1)S(1)}, u32[]{:S(2)}, u32[]{:S(2)}) collective-permute-start(bf16[32,256]{1,0:T(8,128)(2,1)S(1)} %slice.140), channel_id=1, source_target_pairs={{0,1},{1,2},{2,3},{3,4},{4,5},{5,6},{6,7},{7,8},{8,9},{9,10},{10,1... | collective-permute-start | bytes 49160 | tf_op jit(solution)/shard_map/ppermute | solution.py:23
  238.5 3.4 collective-permute-start.3
Sparse Core Ops, SparseCore 0:
  74.0 78.1 reduce-scatter.1
  379.3 175.8 all-reduce.1
where the time goes:
time: 568 us; the launch traced here: 567 us
  waiting for transfers between devices  227 us (40%)
  blocking collectives  218 us (38%)
  matrix products  43.5 us (8%)
  between operations  40.7 us (7%)
  starting transfers between devices  14.5 us (3%)
  local copies, waits for them, and re-layouts  12 us (2%)
  other arithmetic  11.2 us (2%)
    psum x1, waiting for transfers between devices, shards(): basis_grad = lax.psum(partial_value, 'frames') * R ** (-0.5)  176 us
    psum x2, blocking collectives, shards(): squares = lax.psum(jnp.sum(grad * grad), ('frames', 'verts'))  154 us
    reduce_scatter x1, waiting for transfers between devices, shards(): lax.psum_scatter(jnp.dot(err, basis, preferred_element_type=jnp.float32)...  41.6 us
    all_gather x1, blocking collectives, shards(): lax.all_gather(coeffs.astype(jnp.bfloat16), 'verts', axis=0, tiled=True)  33.7 us
    all_gather x1, blocking collectives, shards(): lax.all_gather(coeff.astype(jnp.bfloat16), 'verts', axis=0, tiled=True)  30.7 us
    dot_general x1, matrix products, shards(): jnp.dot(err, basis, preferred_element_type=jnp.float32) * R ** (-0.5)  19.8 us
    dot_general x1, matrix products, residual_rows(): lax.dot_general(coeff_low, basis, (((1,), (1,)), ((), ())), preferred_ele...  19 us
    ppermute x4, starting transfers between devices, shifted(): return lax.ppermute(shard, axis, pairs)  14.4 us
  transfers between devices with their start and end apart: 6, of which 4 were waited for; matrix products, arithmetic and copies ran while one was open for 0% of the time, Pallas kernels for 0%

commit v1 on v0

v1 whole, which is shorter than its diff:
```python
import jax
import jax.numpy as jnp
from jax import lax
from jax.experimental import pallas as pl
from jax.experimental.pallas import tpu as pltpu
from jax.sharding import PartitionSpec as P

R = 256
NLAG = 8
LAGMAX = 32
GRP = 128
ROWS = 1024
COLS = 4096
OWN = 64
NF = 16384
BF = jnp.bfloat16
F32 = jnp.float32
MESH = pl.DeviceIdType.MESH
NT = (((1,), (1,)), ((), ()))
WAVES = 2
WV = 512
SUB = 128


def kernel(
    obs_hbm, maskt_hbm, basis_hbm, coeff_ref, lag_ref, arw_ref,
    newc_ref, newb_hbm,
    obs, mt, mexp, basis, ag, dacc, rs_s, rs_r, ry_s, ry_r, rz_s, rz_r, zpart,
    xe, ge, px, stat1, stat2, mine,
    ct, gbuf, gown, s_opp, r_opp, s_side, r_side, s_z, r_z, nb,
    ld_sem, ag_zs, ag_zr, ag_ys, ag_yr, ag_cs, ag_cr,
    halo_s, halo_r, rc_ss, rc_rs, ry_ss, ry_rs, rz_ss, rz_rs,
    st_s, st_r, opp_s, opp_rs, side_s, side_rs, z_s, z_rs,
    az_s, az_r, ax_s, ax_r, rel_s, rel_r, out_sem,
):
    f = lax.axis_index("frames")
    v = lax.axis_index("verts")
    y, z, c = v // 4, (v // 2) % 2, v % 2
    zl, x = f // 4, f % 4
    glob = f * 16 + v
    has_prev = glob > 0
    has_next = glob < 255
    prev_dev = ((glob + 255) % 256 // 16, (glob + 255) % 16)
    next_dev = ((glob + 1) % 256 // 16, (glob + 1) % 16)

    def vdev(yy, zz, cc):
        return (f, yy * 4 + zz * 2 + cc)

    def fdev(zz, xx):
        return (zz * 4 + xx, v)

    sib = vdev(y, z, 1 - c)
    zpeer = vdev(y, 1 - z, c)
    right = fdev(zl, (x + 1) % 4)
    left = fdev(zl, (x + 3) % 4)

    def remote(src, dst, ssem, rsem, dev):
        return pltpu.make_async_remote_copy(
            src_ref=src, dst_ref=dst, send_sem=ssem, recv_sem=rsem,
            device_id=dev, device_id_type=MESH,
        )

    def load_obs(yy, cc, zz):
        return pltpu.make_async_copy(
            obs_hbm.at[pl.ds(yy * 256 + zz * 128 + cc * 64, 64)],
            obs.at[pl.ds(yy * 256 + cc * 128 + zz * 64, 64)],
            ld_sem.at[0],
        )

    def load_basis():
        return pltpu.make_async_copy(basis_hbm, basis, ld_sem.at[1])

    def load_mask():
        return pltpu.make_async_copy(maskt_hbm, mt, ld_sem.at[2])

    load_mask().start()
    load_basis().start()
    for yy in range(4):
        for cc in range(2):
            for zz in range(2):
                load_obs(yy, cc, zz).start()

    barrier = pltpu.get_barrier_semaphore()

    @pl.loop(1, 16)
    def _(d):
        pl.semaphore_signal(barrier, inc=1, device_id=(f, (v + d) % 16), device_id_type=MESH)
        pl.semaphore_signal(barrier, inc=1, device_id=((f + d) % 16, v), device_id_type=MESH)

    @pl.when(has_prev)
    def _():
        pl.semaphore_signal(barrier, inc=1, device_id=prev_dev, device_id_type=MESH)

    @pl.when(has_next)
    def _():
        pl.semaphore_signal(barrier, inc=1, device_id=next_dev, device_id_type=MESH)

    own = coeff_ref[...]
    ag[0, y, c, z] = (own.astype(BF) * 0.0625).astype(BF)
    xe[32:96] = own

    @pl.when(glob == 0)
    def _():
        xe[0:32] = jnp.zeros((32, R), F32)
        ge[0:32] = jnp.zeros((32, R), F32)

    @pl.when(glob == 255)
    def _():
        xe[96:128] = jnp.zeros((32, R), F32)
        ge[96:128] = jnp.zeros((32, R), F32)

    pl.semaphore_wait(
        barrier, 30 + has_prev.astype(jnp.int32) + has_next.astype(jnp.int32)
    )

    def ag_z(i):
        return remote(ag.at[i, y, c, z], ag.at[i, y, c, z], ag_zs.at[i], ag_zr.at[i], zpeer)

    def ag_y(i, d):
        return remote(
            ag.at[i, y, c], ag.at[i, y, c], ag_ys.at[i, d], ag_yr.at[i, d],
            vdev((y + d) % 4, z, c),
        )

    def ag_y_got(i, d):
        s = (y + 4 - d) % 4
        return remote(ag.at[i, s, c], ag.at[i, s, c], ag_ys.at[i, d], ag_yr.at[i, d], sib)

    def ag_c(i, d):
        s = (y + 4 - d) % 4
        return remote(ag.at[i, s, c], ag.at[i, s, c], ag_cs.at[i, d], ag_cr.at[i, d], sib)

    def halo(buf, i, up):
        if up:
            return remote(
                buf.at[pl.ds(64, 32)], buf.at[pl.ds(0, 32)],
                halo_s.at[i, 0], halo_r.at[i, 0], next_dev,
            )
        return remote(
            buf.at[pl.ds(32, 32)], buf.at[pl.ds(96, 32)],
            halo_s.at[i, 1], halo_r.at[i, 1], prev_dev,
        )

    def halo_start(buf, i):
        @pl.when(has_next)
        def _():
            halo(buf, i, True).start()

        @pl.when(has_prev)
        def _():
            halo(buf, i, False).start()

    def halo_wait(buf, i):
        @pl.when(has_prev)
        def _():
            halo(buf, i, True).wait_recv()

        @pl.when(has_next)
        def _():
            halo(buf, i, False).wait_recv()

    def halo_drain(buf, i):
        @pl.when(has_next)
        def _():
            halo(buf, i, True).wait_send()

        @pl.when(has_prev)
        def _():
            halo(buf, i, False).wait_send()

    def prior(buf):
        full = buf[...]
        r = full[32:128]
        for l in range(NLAG):
            r = r - arw_ref[l : l + 1, :] * pltpu.roll(full, lag_ref[l], 0)[32:128]
        frame = glob * OWN + lax.broadcasted_iota(jnp.int32, (96, R), 0)
        r = jnp.where((frame >= LAGMAX) & (frame < NF), r, 0.0)
        grad = r[0:64]
        for l in range(NLAG):
            grad = grad - arw_ref[l : l + 1, :] * pltpu.roll(r, 96 - lag_ref[l], 0)[0:64]
        return grad

    ag_z(0).start()
    halo_start(xe, 0)

    load_mask().wait()

    def expand(yy):
        for cc in range(2):
            for zz in range(2):
                src = yy * 256 + zz * 128 + cc * 64
                dst = yy * 256 + cc * 128 + zz * 64
                half = mt[:, (src // 128) * 128 : (src // 128) * 128 + 128].astype(F32).T
                m = half[cc * 64 : cc * 64 + 64]
                for g in range(32):
                    mexp[dst : dst + 64, g * 128 : (g + 1) * 128] = jnp.broadcast_to(
                        m[:, g : g + 1], (64, 128)
                    ).astype(BF)

    expand(0)
    ag_z(0).wait_recv()
    for d in range(1, 4):
        ag_y(0, d).start()
    ag_c(0, 0).start()
    for yy in range(1, 4):
        expand(yy)
    halo_wait(xe, 0)
    px[...] = prior(xe)
    load_basis().wait()
    pltpu.make_async_copy(obs_hbm, obs, ld_sem.at[0]).wait()
    for d in range(1, 4):
        ag_y_got(0, d).wait_recv()
        ag_c(0, d).start()

    def rs_core(k):
        return remote(rs_s.at[k], rs_r.at[k], rc_ss.at[k], rc_rs.at[k], sib)

    def rs_y(k):
        return remote(
            ry_s.at[k], ry_r.at[k], ry_ss.at[k], ry_rs.at[k], vdev((y + 4 - k) % 4, z, c)
        )

    @pl.loop(0, 4)
    def _(k):
        ag_c(0, k).wait_recv()
        yy = (y + 4 - k) % 4
        base = pl.multiple_of(yy * 256, 256)
        low = ag[0, yy].reshape(256, R)
        dacc[k] = jnp.zeros((256, R), F32)

        @pl.loop(0, 2)
        def _(jj):
            for u in range(2):
                cols = pl.ds(pl.multiple_of((jj * 2 + u) * 1024, 1024), 1024)
                b = basis[cols, :]
                prod = lax.dot_general(low, b, NT, preferred_element_type=F32)
                e = (prod - obs[pl.ds(base, 256), cols].astype(F32)).astype(BF) * mexp[
                    pl.ds(base, 256), cols
                ]
                dacc[k] += jnp.dot(e, b, preferred_element_type=F32)

        rs_s[k] = dacc[k, pl.ds(pl.multiple_of((1 - c) * 128, 128), 128), :].astype(BF)
        rs_core(k).start()

        @pl.when(k >= 2)
        def _():
            rs_core(k - 1).wait_recv()
            ry_s[k - 1] = (
                dacc[k - 1, pl.ds(pl.multiple_of(c * 128, 128), 128), :]
                + rs_r[k - 1].astype(F32)
            ).astype(BF)
            rs_y(k - 1).start()

    rs_core(3).wait_recv()
    ry_s[3] = (
        dacc[3, pl.ds(pl.multiple_of(c * 128, 128), 128), :] + rs_r[3].astype(F32)
    ).astype(BF)
    rs_y(3).start()
    rs_core(0).wait_recv()
    part = dacc[0, pl.ds(pl.multiple_of(c * 128, 128), 128), :] + rs_r[0].astype(F32)
    for k in range(1, 4):
        rs_y(k).wait_recv()
        part = part + ry_r[k].astype(F32)
    zpart[...] = part
    rz_s[...] = zpart[pl.ds(pl.multiple_of((1 - z) * 64, 64), 64), :].astype(BF)
    rs_z = remote(rz_s, rz_r, rz_ss, rz_rs, zpeer)
    rs_z.start()
    rs_z.wait_recv()
    total = zpart[pl.ds(pl.multiple_of(z * 64, 64), 64), :] + rz_r[...].astype(F32)

    g1 = total * (2.0 ** -12) + px[...]
    ge[32:96] = g1
    halo_start(ge, 1)
    halo_wait(ge, 1)
    pg = prior(ge)
    g1 = ge[32:96]

    def all_sum(val):
        return jnp.sum(jnp.sum(val, axis=0, keepdims=True), axis=1, keepdims=True)

    lane = lax.broadcasted_iota(jnp.int32, (1, 128), 1)
    row = jnp.where(
        lane == 0, all_sum(g1 * g1),
        jnp.where(lane == 1, all_sum(g1 * pg), jnp.where(lane == 2, all_sum(pg * pg), 0.0)),
    )

    def exchange(val, slots, i, at, dev_of):
        mine[i] = val
        slots[at] = val

        @pl.loop(1, 16)
        def _(d):
            remote(mine.at[i], slots.at[at], st_s.at[i], st_r.at[i], dev_of(d)).start()

        def whole():
            return remote(slots.at[pl.ds(0, 15)], slots.at[pl.ds(0, 15)], st_s.at[i], st_r.at[i], sib)

        whole().wait_recv()
        whole().wait_send()
        return jnp.sum(slots[...], axis=0)

    row = exchange(row, stat1, 0, v, lambda d: (f, (v + d) % 16))
    row = exchange(row, stat2, 1, f, lambda d: ((f + d) % 16, v))

    def pick(i):
        return jnp.sum(jnp.where(lane == i, row, 0.0), axis=1, keepdims=True)

    inv = 1.0 / (NF * R)
    ss1, s12, s22 = pick(0), pick(1), pick(2)
    b1 = 0.3 / jnp.sqrt(ss1 * inv + 1e-6)
    ss2 = jnp.maximum(ss1 - 2.0 * b1 * s12 + b1 * b1 * s22, 0.0)
    b2 = 0.3 / jnp.sqrt(ss2 * inv + 1e-6)
    new = coeff_ref[...] - b1 * g1 - b2 * (g1 - b1 * pg)
    newc_ref[...] = new
    ag[1, y, c, z] = (new.astype(BF) * 0.0625).astype(BF)

    ag_z(1).start()
    ag_z(1).wait_recv()
    for d in range(1, 4):
        ag_y(1, d).start()
    ag_c(1, 0).start()
    for d in range(1, 4):
        ag_y_got(1, d).wait_recv()
        ag_c(1, d).start()
    for k in range(4):
        ag_c(1, k).wait_recv()
    for yy in range(4):
        ct[:, yy * 256 : (yy + 1) * 256] = ag[1, yy].reshape(256, R).T

    def opp(w, s):
        half = pl.ds(s * 128, 128)
        return remote(
            s_opp.at[w, half], r_opp.at[w, half], opp_s.at[w, s], opp_rs.at[w, s],
            right if s == 0 else left,
        )

    def side(w, d, h):
        half = pl.ds(h * 128, 128)
        return remote(
            s_side.at[w, d, half], r_side.at[w, d, half],
            side_s.at[w, d, h], side_rs.at[w, d, h], right if d == 0 else left,
        )

    @pl.loop(0, 4 * WAVES)
    def _(n):
        w, role = n // 4, n % 4
        step = jnp.where(role == 0, 2, jnp.where(role == 1, 1, jnp.where(role == 2, 3, 0)))
        xb = (x + step) % 4
        cols = pl.ds(pl.multiple_of(xb * 1024 + w * WV, WV), WV)
        b = basis[cols, :]
        prod = lax.dot_general(ag[1].reshape(ROWS, R), b, NT, preferred_element_type=F32)
        e = (prod - obs[:, cols].astype(F32)).astype(BF) * mexp[:, cols]
        gbuf[role] = jnp.dot(ct[...], e, preferred_element_type=F32)

        @pl.when(role == 0)
        def _():
            s_opp[w] = gbuf[0].astype(BF)
            opp(w, 0).start()
            opp(w, 1).start()

        @pl.when(role == 1)
        def _():
            s_side[w, 0, 128:256] = gbuf[1, 128:256].astype(BF)
            side(w, 0, 1).start()

        @pl.when(role == 2)
        def _():
            s_side[w, 1, 0:128] = gbuf[2, 0:128].astype(BF)
            side(w, 1, 0).start()

        @pl.when(role == 3)
        def _():
            gown[w] = gbuf[3]
            opp(w, 0).wait_recv()
            s_side[w, 0, 0:128] = (gbuf[1, 0:128] + r_opp[w, 0:128].astype(F32)).astype(BF)
            side(w, 0, 0).start()
            opp(w, 1).wait_recv()
            s_side[w, 1, 128:256] = (gbuf[2, 128:256] + r_opp[w, 128:256].astype(F32)).astype(BF)
            side(w, 1, 1).start()

    def zsum(w, d):
        return remote(
            s_z.at[w, d], r_z.at[w, d], z_s.at[w, d], z_rs.at[w, d], fdev((zl + d) % 4, x)
        )

    def rows_of(xx, w, s, lo=0, n=SUB):
        return pl.ds(xx * 1024 + w * WV + s * SUB + lo, n)

    def reduce_x(w):
        for d in range(2):
            for h in range(2):
                side(w, d, h).wait_recv()
        gown[w] = gown[w] + r_side[w, 0].astype(F32) + r_side[w, 1].astype(F32)
        for d in (2, 1, 3):
            s = (zl + d) % 4
            s_z[w, d] = gown[w, :, pl.ds(pl.multiple_of(s * SUB, SUB), SUB)].astype(BF)
            zsum(w, d).start()

    def gather_z(w, d):
        rows = rows_of(x, w, zl)
        return remote(nb.at[rows], nb.at[rows], az_s.at[w, d], az_r.at[w, d], fdev((zl + d) % 4, x))

    def gather_z_got(w, d):
        rows = rows_of(x, w, (zl + 4 - d) % 4)
        return remote(nb.at[rows], nb.at[rows], az_s.at[w, d], az_r.at[w, d], left)

    def gather_x(w, d, t):
        rows = rows_of(x, w, (zl + 4 - d) % 4)
        return remote(
            nb.at[rows], nb.at[rows], ax_s.at[w, d, t], ax_r.at[w, d, t],
            right if t == 0 else left,
        )

    def gather_x_got(w, d, t):
        rows = rows_of((x + (3 if t == 0 else 1)) % 4, w, (zl + 4 - d) % 4)
        return remote(nb.at[rows], nb.at[rows], ax_s.at[w, d, t], ax_r.at[w, d, t], left)

    def relay(w, d, t):
        rows = rows_of((x + (3 if t == 0 else 1)) % 4, w, (zl + 4 - d) % 4, 64 * t, 64)
        return remote(
            nb.at[rows], nb.at[rows], rel_s.at[w, d, t], rel_r.at[w, d, t],
            right if t == 0 else left,
        )

    def relay_got(w, d, t):
        rows = rows_of((x + 2) % 4, w, (zl + 4 - d) % 4, 64 * t, 64)
        return remote(nb.at[rows], nb.at[rows], rel_s.at[w, d, t], rel_r.at[w, d, t], left)

    def update(w):
        acc = gown[w, :, pl.ds(pl.multiple_of(zl * SUB, SUB), SUB)]
        for d in range(1, 4):
            zsum(w, d).wait_recv()
            acc = acc + r_z[w, d].astype(F32)
        rows = pl.ds(pl.multiple_of(x * 1024 + w * WV + zl * SUB, SUB), SUB)
        nb[rows, :] = (basis[rows, :].astype(F32) - (2.0 ** -6) * acc.T).astype(BF)
        for d in (2, 1, 3):
            gather_z(w, d).start()
        gather_x(w, 0, 0).start()
        gather_x(w, 0, 1).start()

    def spread(w):
        for d in range(1, 4):
            gather_z_got(w, d).wait_recv()
            gather_x(w, d, 0).start()
            gather_x(w, d, 1).start()

    def pass_on(w):
        for d in range(4):
            for t in range(2):
                gather_x_got(w, d, t).wait_recv()
                relay(w, d, t).start()

    reduce_x(0)
    update(0)
    spread(0)
    reduce_x(1)
    pass_on(0)
    update(1)
    spread(1)
    pass_on(1)
    for w in range(WAVES):
        for d in range(4):
            for t in range(2):
                relay_got(w, d, t).wait_recv()
    store = pltpu.make_async_copy(nb, newb_hbm, out_sem)
    store.start()

    for i in range(2):
        ag_z(i).wait_send()
        for d in range(1, 4):
            ag_y(i, d).wait_send()
        for d in range(4):
            ag_c(i, d).wait_send()
    halo_drain(xe, 0)
    halo_drain(ge, 1)
    for k in range(4):
        rs_core(k).wait_send()
        if k:
            rs_y(k).wait_send()
    rs_z.wait_send()
    for w in range(WAVES):
        for s in range(2):
            opp(w, s).wait_send()
            for h in range(2):
                side(w, s, h).wait_send()
        for d in range(4):
            if d:
                zsum(w, d).wait_send()
                gather_z(w, d).wait_send()
            for t in range(2):
                gather_x(w, d, t).wait_send()
                relay(w, d, t).wait_send()
    store.wait()


def shards(observed, mask, basis, coeffs, lag_set, ar_weight):
    vm = pltpu.VMEM
    dma = pltpu.SemaphoreType.DMA
    scratch = [
        vm((ROWS, COLS), BF),
        vm((32, ROWS), jnp.int32),
        vm((ROWS, COLS), BF),
        vm((COLS, R), BF),
        vm((2, 4, 2, 2, OWN, R), BF),
        vm((4, 256, R), F32),
        vm((4, 128, R), BF),
        vm((4, 128, R), BF),
        vm((4, 128, R), BF),
        vm((4, 128, R), BF),
        vm((OWN, R), BF),
        vm((OWN, R), BF),
        vm((128, R), F32),
        vm((128, R), F32),
        vm((128, R), F32),
        vm((OWN, R), F32),
        vm((16, 1, 128), F32),
        vm((16, 1, 128), F32),
        vm((2, 1, 128), F32),
        vm((R, ROWS), BF),
        vm((4, R, WV), F32),
        vm((WAVES, R, WV), F32),
        vm((WAVES, R, WV), BF),
        vm((WAVES, R, WV), BF),
        vm((WAVES, 2, R, WV), BF),
        vm((WAVES, 2, R, WV), BF),
        vm((WAVES, 4, R, SUB), BF),
        vm((WAVES, 4, R, SUB), BF),
        vm((COLS, R), BF),
        dma((3,)),
        dma((2,)), dma((2,)), dma((2, 4)), dma((2, 4)), dma((2, 4)), dma((2, 4)),
        dma((2, 2)), dma((2, 2)), dma((4,)), dma((4,)), dma((4,)), dma((4,)),
        dma, dma,
        dma((2,)), dma((2,)),
        dma((WAVES, 2)), dma((WAVES, 2)), dma((WAVES, 2, 2)), dma((WAVES, 2, 2)),
        dma((WAVES, 4)), dma((WAVES, 4)), dma((WAVES, 4)), dma((WAVES, 4)),
        dma((WAVES, 4, 2)), dma((WAVES, 4, 2)), dma((WAVES, 4, 2)), dma((WAVES, 4, 2)),
        dma,
    ]
    anyspace = pl.BlockSpec(memory_space=pl.ANY)
    vmem = pl.BlockSpec(memory_space=pltpu.VMEM)
    return pl.pallas_call(
        kernel,
        out_shape=(
            jax.ShapeDtypeStruct((OWN, R), F32),
            jax.ShapeDtypeStruct((COLS, R), BF),
        ),
        in_specs=[anyspace, anyspace, anyspace, vmem, pl.BlockSpec(memory_space=pltpu.SMEM), vmem],
        out_specs=(vmem, anyspace),
        scratch_shapes=scratch,
        compiler_params=pltpu.CompilerParams(
            collective_id=0, has_side_effects=True, vmem_limit_bytes=60 * 2**20
        ),
        name="alternation",
    )(observed, mask.T, basis, coeffs, lag_set, ar_weight)


def solution(mesh):
    placed = (
        P("frames", "verts"),
        P("frames", "verts"),
        P("verts", None),
        P(("frames", "verts"), None),
        P(),
        P(),
    )
    return jax.shard_map(
        shards,
        mesh=mesh,
        in_specs=placed,
        out_specs=(P(("frames", "verts"), None), P("verts", None)),
        check_vma=False,
    )
```

time: 568 us -> 125 us (0.22)
  waiting for transfers between devices: 227 us -> 0 us
  blocking collectives: 218 us -> 0 us
  Pallas kernels: 0 us -> 118 us
  matrix products: 43.5 us -> 0 us
  between operations: 40.7 us -> 0.64 us
  starting transfers between devices: 14.5 us -> 0 us
  other arithmetic: 11.2 us -> 0 us
  local copies, waits for them, and re-layouts: 12 us -> 4.52 us
    psum x1 -> x0, waiting for transfers between devices: 176 us -> none  [shards(): basis_grad = lax.psum(partial_value, 'frames') * R ** (-0.5)]
    psum x2 -> x0, blocking collectives: 154 us -> none  [shards(): squares = lax.psum(jnp.sum(grad * grad), ('frames', 'verts'))]
    pallas_call x0 -> x1, Pallas kernels: none -> 118 us  [shards(): pl.pallas_call(kernel, out_shape=(jax.ShapeDtypeStruct((OWN, R), F32), ja...]
    all_gather x2 -> x0, blocking collectives: 64.3 us -> none  [the longest x1 33.7 us: shards(): lax.all_gather(coeffs.astype(jnp.bfloat16), 'verts', axis=0, tiled=True)]
    dot_general x3 -> x0, matrix products: 43.5 us -> none  [the longest x1 19.8 us: shards(): jnp.dot(err, basis, preferred_element_type=jnp.float32) * R ** (-0.5)]
    reduce_scatter x1 -> x0, waiting for transfers between devices: 41.6 us -> none  [shards(): lax.psum_scatter(jnp.dot(err, basis, preferred_element_type=jnp.float32)...]
    ppermute x4 -> x0, starting transfers between devices: 14.4 us -> none  [shifted(): return lax.ppermute(shard, axis, pairs)]
    mul x1 -> x0, local copies, waits for them, and re-layouts: 11.1 us -> none  [residual_rows(): diff.reshape(rows, mask_rows.shape[1], GRP)]
  transfers between devices with their start and end apart: 6 -> 0, of which waited for: 4 -> 0; matrix products, arithmetic and copies ran while one was open for 0% -> 0% of each run, Pallas kernels for 0% -> 0%
where the time goes in v1:
time: 125 us; the launch traced here: 123 us
  Pallas kernels  118 us (94%)
  local copies, waits for them, and re-layouts  4.52 us (4%)
    pallas_call x1, Pallas kernels, shards(): pl.pallas_call(kernel, out_shape=(jax.ShapeDtypeStruct((OWN, R), F32), ja...  118 us
    unnamed x2, local copies, waits for them, and re-layouts  4.52 us

profile of v1, /device:TPU:16, one launch (start us, length us, event | category | flops | bytes accessed | tf_op | source)
XLA Modules:
  0.0 123.4 jit_solution(11339555241882285285)
XLA Ops:
  0.6 118.2 %alternation.1 = (f32[64,256]{1,0:T(8,128)}, bf16[4096,256]{1,0:T(8,128)(2,1)}) custom-call(bf16[1024,4096]{1,0:T(8,128)(2,1)} %obs_hbm.1, s32[32,1024]{1,0:T(8,128)} %bitcast.1, bf16[4096,256]{1,0:T(8,128)(2,1)} %basis_hbm.1, f32[64,256]{1,0:T(8,128)} %coeff_ref.1, s32[8]{0:T(128)} %lag_ref.1, f32[8,256]{1,0:T(8,128)} %arw_ref.1), custom_call_target="tpu_custom_call" | custom-call | tf_op jit(solution)/shard_map/alternation/pallas_call | solution.py:541
  118.9 1.5 %copy.10 = f32[64,256]{1,0:T(8,128)} copy(f32[64,256]{1,0:T(8,128)} %get-tuple-element.4) | data formatting | bytes 131072
  120.3 3.0 %copy.11 = bf16[4096,256]{1,0:T(8,128)(2,1)} copy(bf16[4096,256]{1,0:T(8,128)(2,1)} %get-tuple-element.5) | data formatting | bytes 4194304

commit v2 on v1

v2 whole, which is shorter than its diff:
```python
import jax
import jax.numpy as jnp
from jax import lax
from jax.experimental import pallas as pl
from jax.experimental.pallas import tpu as pltpu
from jax.sharding import PartitionSpec as P

R = 256
NLAG = 8
LAGMAX = 32
GRP = 128
ROWS = 1024
COLS = 4096
OWN = 64
NF = 16384
BF = jnp.bfloat16
F32 = jnp.float32
MESH = pl.DeviceIdType.MESH
NT = (((1,), (1,)), ((), ()))
WAVES = 4
WV = 256
SUB = 128


def kernel(
    obs_hbm, maskt_hbm, basis_hbm, coeff_ref, lag_ref, arw_ref,
    newc_ref, newb_hbm,
    obs, mt, mexp, basis, ag, dacc, rs_s, rs_r, ry_s, ry_r, rz_s, rz_r, zpart,
    xe, px, gfull, ghalo, pgb, cn, stat1, stat2, mine,
    ct, gacc, gown, s_opp, r_opp, s_side, r_side, s_z, r_z, nb,
    ld_sem, ag_zs, ag_zr, ag_ys, ag_yr, ag_cs, ag_cr,
    halo_s, halo_r, gh_s, gh_r, rc_ss, rc_rs, ry_ss, ry_rs, rz_ss, rz_rs,
    st_s, st_r, opp_s, opp_rs, side_s, side_rs, z_s, z_rs,
    az_s, az_r, ax_s, ax_r, rel_s, rel_r, out_sem,
):
    f = lax.axis_index("frames")
    v = lax.axis_index("verts")
    y, z, c = v // 4, (v // 2) % 2, v % 2
    zl, x = f // 4, f % 4
    glob = f * 16 + v
    has_prev = glob > 0
    has_next = glob < 255
    prev_dev = ((glob + 255) % 256 // 16, (glob + 255) % 16)
    next_dev = ((glob + 1) % 256 // 16, (glob + 1) % 16)

    below = ((f + 15) % 16, v)
    above = ((f + 1) % 16, v)

    def vdev(yy, zz, cc):
        return (f, yy * 4 + zz * 2 + cc)

    def fdev(zz, xx):
        return (zz * 4 + xx, v)

    sib = vdev(y, z, 1 - c)
    zpeer = vdev(y, 1 - z, c)
    right = fdev(zl, (x + 1) % 4)
    left = fdev(zl, (x + 3) % 4)

    def remote(src, dst, ssem, rsem, dev):
        return pltpu.make_async_remote_copy(
            src_ref=src, dst_ref=dst, send_sem=ssem, recv_sem=rsem,
            device_id=dev, device_id_type=MESH,
        )

    def load_obs(yy, cc, zz):
        return pltpu.make_async_copy(
            obs_hbm.at[pl.ds(yy * 256 + zz * 128 + cc * 64, 64)],
            obs.at[pl.ds(yy * 256 + cc * 128 + zz * 64, 64)],
            ld_sem.at[0],
        )

    def load_basis():
        return pltpu.make_async_copy(basis_hbm, basis, ld_sem.at[1])

    def load_mask():
        return pltpu.make_async_copy(maskt_hbm, mt, ld_sem.at[2])

    load_mask().start()
    load_basis().start()
    for yy in range(4):
        for cc in range(2):
            for zz in range(2):
                load_obs(yy, cc, zz).start()

    barrier = pltpu.get_barrier_semaphore()

    for d in range(1, 4):
        for dev in (vdev((y + d) % 4, z, c), fdev(zl, (x + d) % 4), fdev((zl + d) % 4, x)):
            pl.semaphore_signal(barrier, inc=1, device_id=dev, device_id_type=MESH)
    for dev in (zpeer, sib):
        pl.semaphore_signal(barrier, inc=1, device_id=dev, device_id_type=MESH)
    for has, dev in (
        (has_prev, prev_dev), (has_next, next_dev), (f > 0, below), (f < 15, above)
    ):

        @pl.when(has)
        def _():
            pl.semaphore_signal(barrier, inc=1, device_id=dev, device_id_type=MESH)

    own = coeff_ref[...]
    ag[0, y, c, z] = (own.astype(BF) * 0.0625).astype(BF)
    xe[32:96] = own

    @pl.when(glob == 0)
    def _():
        xe[0:32] = jnp.zeros((32, R), F32)

    @pl.when(glob == 255)
    def _():
        xe[96:128] = jnp.zeros((32, R), F32)

    @pl.when(f == 0)
    def _():
        ghalo[0] = jnp.zeros((32, R), BF)

    @pl.when(f == 15)
    def _():
        ghalo[1] = jnp.zeros((32, R), BF)

    def expand(k):
        yy = (y + 4 - k) % 4
        for zz in range(2):
            src = pl.multiple_of(yy * 256 + zz * 128, 128)
            m = mt[:, pl.ds(src, 128)].astype(F32).T
            for cc in range(2):
                dst = pl.multiple_of(yy * 256 + cc * 128 + zz * 64, 64)
                for g in range(32):
                    mexp[pl.ds(dst, 64), g * 128 : (g + 1) * 128] = jnp.broadcast_to(
                        m[cc * 64 : cc * 64 + 64, g : g + 1], (64, 128)
                    ).astype(BF)

    load_mask().wait()
    expand(0)
    expand(1)
    pl.semaphore_wait(
        barrier,
        11 + has_prev.astype(jnp.int32) + has_next.astype(jnp.int32)
        + (f > 0).astype(jnp.int32) + (f < 15).astype(jnp.int32),
    )

    def ag_z(i):
        return remote(ag.at[i, y, c, z], ag.at[i, y, c, z], ag_zs.at[i], ag_zr.at[i], zpeer)

    def ag_y(i, d):
        return remote(
            ag.at[i, y, c], ag.at[i, y, c], ag_ys.at[i, d], ag_yr.at[i, d],
            vdev((y + d) % 4, z, c),
        )

    def ag_y_got(i, d):
        s = (y + 4 - d) % 4
        return remote(ag.at[i, s, c], ag.at[i, s, c], ag_ys.at[i, d], ag_yr.at[i, d], sib)

    def ag_c(i, d):
        s = (y + 4 - d) % 4
        return remote(ag.at[i, s, c], ag.at[i, s, c], ag_cs.at[i, d], ag_cr.at[i, d], sib)

    def halo(up):
        if up:
            return remote(
                xe.at[pl.ds(64, 32)], xe.at[pl.ds(0, 32)], halo_s.at[0], halo_r.at[0], next_dev
            )
        return remote(
            xe.at[pl.ds(32, 32)], xe.at[pl.ds(96, 32)], halo_s.at[1], halo_r.at[1], prev_dev
        )

    def ghalo_copy(up):
        if up:
            return remote(
                ag.at[1, 3, 1, 1, pl.ds(32, 32)], ghalo.at[0], gh_s.at[0], gh_r.at[0], above
            )
        return remote(ag.at[1, 0, 0, 0, pl.ds(0, 32)], ghalo.at[1], gh_s.at[1], gh_r.at[1], below)

    def ends(copy, lower, upper, act):
        @pl.when(upper)
        def _():
            d = copy(act != "recv")
            d.start() if act == "start" else d.wait_recv() if act == "recv" else d.wait_send()

        @pl.when(lower)
        def _():
            d = copy(act == "recv")
            d.start() if act == "start" else d.wait_recv() if act == "recv" else d.wait_send()

    def prior(window, n, first):
        m = n + 32
        r = window[32:]
        for l in range(NLAG):
            r = r - arw_ref[l : l + 1, :] * pltpu.roll(window, lag_ref[l], 0)[32:]
        frame = first + lax.broadcasted_iota(jnp.int32, (m, R), 0)
        r = jnp.where((frame >= LAGMAX) & (frame < NF), r, 0.0)
        grad = r[0:n]
        for l in range(NLAG):
            grad = grad - arw_ref[l : l + 1, :] * pltpu.roll(r, m - lag_ref[l], 0)[0:n]
        return grad

    ag_z(0).start()
    ends(halo, has_prev, has_next, "start")
    ag_z(0).wait_recv()
    for d in range(1, 4):
        ag_y(0, d).start()
    ag_c(0, 0).start()
    expand(2)
    expand(3)
    ends(halo, has_prev, has_next, "recv")
    px[...] = prior(xe[...], OWN, glob * OWN)
    load_basis().wait()
    pltpu.make_async_copy(obs_hbm, obs, ld_sem.at[0]).wait()

    def rs_core(k):
        return remote(rs_s.at[k], rs_r.at[k], rc_ss.at[k], rc_rs.at[k], sib)

    def rs_y(k):
        return remote(
            ry_s.at[k], ry_r.at[k], ry_ss.at[k], ry_rs.at[k], vdev((y + 4 - k) % 4, z, c)
        )

    @pl.loop(0, 4)
    def _(k):
        ag_c(0, k).wait_recv()
        yy = (y + 4 - k) % 4
        base = pl.multiple_of(yy * 256, 256)
        low = ag[0, yy].reshape(256, R)
        dacc[k] = jnp.zeros((256, R), F32)

        @pl.loop(0, 2)
        def _(jj):
            for u in range(2):
                cols = pl.ds(pl.multiple_of((jj * 2 + u) * 1024, 1024), 1024)
                b = basis[cols, :]
                prod = lax.dot_general(low, b, NT, preferred_element_type=F32)
                e = (prod - obs[pl.ds(base, 256), cols].astype(F32)).astype(BF) * mexp[
                    pl.ds(base, 256), cols
                ]
                dacc[k] += jnp.dot(e, b, preferred_element_type=F32)

        rs_s[k] = dacc[k, pl.ds(pl.multiple_of((1 - c) * 128, 128), 128), :].astype(BF)
        rs_core(k).start()

        @pl.when(k == 0)
        def _():
            for d in range(1, 4):
                ag_y_got(0, d).wait_recv()
                ag_c(0, d).start()

        @pl.when(k >= 2)
        def _():
            rs_core(k - 1).wait_recv()
            ry_s[k - 1] = (
                dacc[k - 1, pl.ds(pl.multiple_of(c * 128, 128), 128), :]
                + rs_r[k - 1].astype(F32)
            ).astype(BF)
            rs_y(k - 1).start()

    rs_core(3).wait_recv()
    ry_s[3] = (
        dacc[3, pl.ds(pl.multiple_of(c * 128, 128), 128), :] + rs_r[3].astype(F32)
    ).astype(BF)
    rs_y(3).start()
    rs_core(0).wait_recv()
    part = dacc[0, pl.ds(pl.multiple_of(c * 128, 128), 128), :] + rs_r[0].astype(F32)
    for k in range(1, 4):
        rs_y(k).wait_recv()
        part = part + ry_r[k].astype(F32)
    zpart[...] = part * (2.0 ** -12)
    mine_rows = pl.ds(pl.multiple_of(z * 64, 64), 64)
    zpart[mine_rows, :] += px[...]
    rz_s[...] = zpart[...].astype(BF)
    rs_z = remote(rz_s, rz_r, rz_ss, rz_rs, zpeer)
    rs_z.start()
    rs_z.wait_recv()

    g128 = zpart[...] + rz_r[...].astype(F32)
    zpart[...] = g128
    ag[1, y, c] = g128.astype(BF).reshape(2, OWN, R)
    for d in range(1, 4):
        ag_y(1, d).start()
    ag_c(1, 0).start()
    for d in range(1, 4):
        ag_y_got(1, d).wait_recv()
        ag_c(1, d).start()
    for k in range(4):
        ag_c(1, k).wait_recv()
    ends(ghalo_copy, f > 0, f < 15, "start")
    for yy in range(4):
        for cc in range(2):
            for zz in range(2):
                at = 32 + yy * 256 + zz * 128 + cc * 64
                gfull[at : at + 64] = ag[1, yy, cc, zz].astype(F32)

    def fold(val):
        return jnp.sum(val, axis=0, keepdims=True)

    sums = [jnp.zeros((1, R), F32)] * 3
    for k in (1, 2, 0, 3):
        if k == 0:
            ends(ghalo_copy, f > 0, f < 15, "recv")
            gfull[0:32] = ghalo[0].astype(F32)
            gfull[1056:1088] = ghalo[1].astype(F32)
        window = gfull[k * 256 : k * 256 + 320]
        p = prior(window, 256, f * ROWS + k * 256)
        pgb[k * 256 : (k + 1) * 256] = p
        g = window[32:288]
        sums = [sums[0] + fold(g * g), sums[1] + fold(g * p), sums[2] + fold(p * p)]

    lane = lax.broadcasted_iota(jnp.int32, (1, 128), 1)
    s1, s12, s2 = [jnp.sum(t, axis=1, keepdims=True) for t in sums]
    row = jnp.where(
        lane == 0, s1, jnp.where(lane == 1, s12, jnp.where(lane == 2, s2, 0.0))
    )

    def exchange(val, slots, i, at, dev_of):
        mine[i] = val
        slots[at] = val
        for d in range(1, 4):
            remote(mine.at[i], slots.at[at], st_s.at[i], st_r.at[i], dev_of(d)).start()

        def whole():
            return remote(slots.at[pl.ds(0, 3)], slots.at[pl.ds(0, 3)], st_s.at[i], st_r.at[i], sib)

        whole().wait_recv()
        whole().wait_send()
        return jnp.sum(slots[...], axis=0)

    row = exchange(row, stat1, 0, x, lambda d: fdev(zl, (x + d) % 4))
    row = exchange(row, stat2, 1, zl, lambda d: fdev((zl + d) % 4, x))

    def pick(i):
        return jnp.sum(jnp.where(lane == i, row, 0.0), axis=1, keepdims=True)

    inv = 1.0 / (NF * R)
    ss1, s12, s22 = pick(0), pick(1), pick(2)
    b1 = 0.3 / jnp.sqrt(ss1 * inv + 1e-6)
    ss2 = jnp.maximum(ss1 - 2.0 * b1 * s12 + b1 * b1 * s22, 0.0)
    b2 = 0.3 / jnp.sqrt(ss2 * inv + 1e-6)
    by_g, by_p = b1 + b2, b1 * b2
    for yy in range(4):
        for cc in range(2):
            for zz in range(2):
                at = yy * 256 + zz * 128 + cc * 64
                low = ag[0, yy, cc, zz].astype(F32) - 0.0625 * (
                    by_g * gfull[32 + at : 96 + at] - by_p * pgb[at : at + 64]
                )
                to = yy * 256 + cc * 128 + zz * 64
                cn[to : to + 64] = low.astype(BF)
        ct[:, yy * 256 : (yy + 1) * 256] = cn[yy * 256 : (yy + 1) * 256].T
    own_at = pl.multiple_of(v * OWN, OWN)
    newc_ref[...] = (
        coeff_ref[...] - by_g * zpart[mine_rows, :] + by_p * pgb[pl.ds(own_at, OWN), :]
    )

    def opp(w, s):
        half = pl.ds(s * 128, 128)
        return remote(
            s_opp.at[w, half], r_opp.at[w, half], opp_s.at[w, s], opp_rs.at[w, s],
            right if s == 0 else left,
        )

    def side(w, d, h):
        half = pl.ds(h * 128, 128)
        return remote(
            s_side.at[w, d, half], r_side.at[w, d, half],
            side_s.at[w, d, h], side_rs.at[w, d, h], right if d == 0 else left,
        )

    def two_blocks(w, xa, xb):
        def both(ref):
            return jnp.concatenate(
                [ref[:, pl.ds(pl.multiple_of(t * 1024 + w * WV, WV), WV)] for t in (xa, xb)], axis=1
            )

        b = jnp.concatenate(
            [basis[pl.ds(pl.multiple_of(t * 1024 + w * WV, WV), WV), :] for t in (xa, xb)], axis=0
        )
        prod = lax.dot_general(cn[...], b, NT, preferred_element_type=F32)
        e = (prod - both(obs).astype(F32)).astype(BF) * both(mexp)
        return jnp.dot(ct[...], e, preferred_element_type=F32)

    def compute(w):
        g = two_blocks(w, (x + 2) % 4, (x + 1) % 4)
        s_opp[w] = g[:, 0:WV].astype(BF)
        opp(w, 0).start()
        opp(w, 1).start()
        s_side[w, 0, 128:256] = g[128:256, WV:].astype(BF)
        side(w, 0, 1).start()
        gacc[w, 0] = g[0:128, WV:]
        g = two_blocks(w, (x + 3) % 4, x)
        s_side[w, 1, 0:128] = g[0:128, 0:WV].astype(BF)
        side(w, 1, 0).start()
        gacc[w, 1] = g[128:256, 0:WV]
        gown[w] = g[:, WV:]

    def join(w):
        opp(w, 0).wait_recv()
        s_side[w, 0, 0:128] = (gacc[w, 0] + r_opp[w, 0:128].astype(F32)).astype(BF)
        side(w, 0, 0).start()
        opp(w, 1).wait_recv()
        s_side[w, 1, 128:256] = (gacc[w, 1] + r_opp[w, 128:256].astype(F32)).astype(BF)
        side(w, 1, 1).start()

    def zsum(w, d):
        return remote(
            s_z.at[w, d], r_z.at[w, d], z_s.at[w, d], z_rs.at[w, d], fdev((zl + d) % 4, x)
        )

    def quarter(s):
        return (
            pl.ds(pl.multiple_of(s // 2 * SUB, SUB), SUB),
            pl.ds(pl.multiple_of(s % 2 * SUB, SUB), SUB),
        )

    def reduce_x(w):
        for d in range(2):
            for h in range(2):
                side(w, d, h).wait_recv()
        gown[w] = gown[w] + r_side[w, 0].astype(F32) + r_side[w, 1].astype(F32)
        for d in (2, 1, 3):
            ranks, verts = quarter((zl + d) % 4)
            s_z[w, d] = gown[w, ranks, verts].astype(BF)
            zsum(w, d).start()

    def quarter_of(w, s):
        return nb.at[s // 2, pl.ds(pl.multiple_of(x * 1024 + w * WV + s % 2 * SUB, SUB), SUB)]

    def block_of(w, xx):
        return nb.at[:, pl.ds(pl.multiple_of(xx * 1024 + w * WV, WV), WV)]

    def half_of(w, xx, t):
        return nb.at[t, pl.ds(pl.multiple_of(xx * 1024 + w * WV, WV), WV)]

    def gather_z(w, d):
        part = quarter_of(w, zl)
        return remote(part, part, az_s.at[w, d], az_r.at[w, d], fdev((zl + d) % 4, x))

    def gather_z_got(w, d):
        part = quarter_of(w, (zl + 4 - d) % 4)
        return remote(part, part, az_s.at[w, d], az_r.at[w, d], left)

    def gather_x(w, t):
        part = block_of(w, x)
        return remote(part, part, ax_s.at[w, t], ax_r.at[w, t], right if t == 0 else left)

    def gather_x_got(w, t):
        part = block_of(w, (x + (3 if t == 0 else 1)) % 4)
        return remote(part, part, ax_s.at[w, t], ax_r.at[w, t], left)

    def relay(w, t):
        part = half_of(w, (x + (3 if t == 0 else 1)) % 4, t)
        return remote(part, part, rel_s.at[w, t], rel_r.at[w, t], right if t == 0 else left)

    def relay_got(w, t):
        part = half_of(w, (x + 2) % 4, t)
        return remote(part, part, rel_s.at[w, t], rel_r.at[w, t], left)

    def store(w, xx, t):
        rows = pl.ds(xx * 1024 + w * WV, WV)
        return pltpu.make_async_copy(
            nb.at[t, rows], newb_hbm.at[rows, pl.ds(t * 128, 128)], out_sem.at[w, xx, t]
        )

    def update(w):
        ranks, verts = quarter(zl)
        acc = gown[w, ranks, verts]
        for d in range(1, 4):
            zsum(w, d).wait_recv()
            acc = acc + r_z[w, d].astype(F32)
        rows = pl.ds(pl.multiple_of(x * 1024 + w * WV + zl % 2 * SUB, SUB), SUB)
        nb[zl // 2, rows, :] = (
            basis[rows, ranks].astype(F32) - (2.0 ** -6) * acc.T
        ).astype(BF)
        for d in (2, 1, 3):
            gather_z(w, d).start()

    def spread(w):
        for d in range(1, 4):
            gather_z_got(w, d).wait_recv()
        gather_x(w, 0).start()
        gather_x(w, 1).start()

    def pass_on(w):
        for t in range(2):
            gather_x_got(w, t).wait_recv()
            relay(w, t).start()

    def finish(w):
        for t in range(2):
            relay_got(w, t).wait_recv()
        for xx in range(4):
            for t in range(2):
                store(w, xx, t).start()

    for act, w in (
        (compute, 0), (compute, 1), (join, 0), (compute, 2), (join, 1), (reduce_x, 0),
        (compute, 3), (join, 2), (update, 0), (reduce_x, 1), (join, 3), (spread, 0),
        (update, 1), (reduce_x, 2), (spread, 1), (reduce_x, 3), (update, 2), (pass_on, 0),
        (update, 3), (spread, 2), (pass_on, 1), (spread, 3), (finish, 0), (pass_on, 2),
        (finish, 1), (pass_on, 3), (finish, 2), (finish, 3),
    ):
        act(w)

    ag_z(0).wait_send()
    for i in range(2):
        for d in range(1, 4):
            ag_y(i, d).wait_send()
        for d in range(4):
            ag_c(i, d).wait_send()
    ends(halo, has_prev, has_next, "send")
    ends(ghalo_copy, f > 0, f < 15, "send")
    for k in range(4):
        rs_core(k).wait_send()
        if k:
            rs_y(k).wait_send()
    rs_z.wait_send()
    for w in range(WAVES):
        for t in range(2):
            opp(w, t).wait_send()
            for h in range(2):
                side(w, t, h).wait_send()
            gather_x(w, t).wait_send()
            relay(w, t).wait_send()
        for d in range(1, 4):
            zsum(w, d).wait_send()
            gather_z(w, d).wait_send()
    for w in range(WAVES):
        for xx in range(4):
            for t in range(2):
                store(w, xx, t).wait()


def shards(observed, mask, basis, coeffs, lag_set, ar_weight):
    vm = pltpu.VMEM
    dma = pltpu.SemaphoreType.DMA
    scratch = [
        vm((ROWS, COLS), BF),
        vm((32, ROWS), jnp.int32),
        vm((ROWS, COLS), BF),
        vm((COLS, R), BF),
        vm((2, 4, 2, 2, OWN, R), BF),
        vm((4, 256, R), F32),
        vm((4, 128, R), BF),
        vm((4, 128, R), BF),
        vm((4, 128, R), BF),
        vm((4, 128, R), BF),
        vm((128, R), BF),
        vm((128, R), BF),
        vm((128, R), F32),
        vm((128, R), F32),
        vm((OWN, R), F32),
        vm((ROWS + 64, R), F32),
        vm((2, 32, R), BF),
        vm((ROWS, R), F32),
        vm((ROWS, R), BF),
        vm((4, 1, 128), F32),
        vm((4, 1, 128), F32),
        vm((2, 1, 128), F32),
        vm((R, ROWS), BF),
        vm((WAVES, 2, 128, WV), F32),
        vm((WAVES, R, WV), F32),
        vm((WAVES, R, WV), BF),
        vm((WAVES, R, WV), BF),
        vm((WAVES, 2, R, WV), BF),
        vm((WAVES, 2, R, WV), BF),
        vm((WAVES, 4, SUB, SUB), BF),
        vm((WAVES, 4, SUB, SUB), BF),
        vm((2, COLS, 128), BF),
        dma((3,)),
        dma((2,)), dma((2,)), dma((2, 4)), dma((2, 4)), dma((2, 4)), dma((2, 4)),
        dma((2,)), dma((2,)), dma((2,)), dma((2,)),
        dma((4,)), dma((4,)), dma((4,)), dma((4,)), dma, dma,
        dma((2,)), dma((2,)),
        dma((WAVES, 2)), dma((WAVES, 2)), dma((WAVES, 2, 2)), dma((WAVES, 2, 2)),
        dma((WAVES, 4)), dma((WAVES, 4)), dma((WAVES, 4)), dma((WAVES, 4)),
        dma((WAVES, 2)), dma((WAVES, 2)), dma((WAVES, 2)), dma((WAVES, 2)),
        dma((WAVES, 4, 2)),
    ]
    anyspace = pl.BlockSpec(memory_space=pl.ANY)
    vmem = pl.BlockSpec(memory_space=pltpu.VMEM)
    return pl.pallas_call(
        kernel,
        out_shape=(
            jax.ShapeDtypeStruct((OWN, R), F32),
            jax.ShapeDtypeStruct((COLS, R), BF),
        ),
        in_specs=[anyspace, anyspace, anyspace, vmem, pl.BlockSpec(memory_space=pltpu.SMEM), vmem],
        out_specs=(vmem, anyspace),
        scratch_shapes=scratch,
        compiler_params=pltpu.CompilerParams(
            collective_id=0, has_side_effects=True, vmem_limit_bytes=60 * 2**20
        ),
        name="alternation",
    )(observed, mask.T, basis, coeffs, lag_set, ar_weight)


def solution(mesh):
    placed = (
        P("frames", "verts"),
        P("frames", "verts"),
        P("verts", None),
        P(("frames", "verts"), None),
        P(),
        P(),
    )
    return jax.shard_map(
        shards,
        mesh=mesh,
        in_specs=placed,
        out_specs=(P(("frames", "verts"), None), P("verts", None)),
        check_vma=False,
    )
```

time: 125 us -> 114 us (0.912)
  Pallas kernels: 118 us -> 108 us
    pallas_call x1, Pallas kernels: 118 us -> 108 us  [shards(): pl.pallas_call(kernel, out_shape=(jax.ShapeDtypeStruct((OWN, R), F32), ja...]
where the time goes in v2:
time: 114 us; the launch traced here: 113 us
  Pallas kernels  108 us (95%)
  local copies, waits for them, and re-layouts  4.52 us (4%)
    pallas_call x1, Pallas kernels, shards(): pl.pallas_call(kernel, out_shape=(jax.ShapeDtypeStruct((OWN, R), F32), ja...  108 us
    unnamed x2, local copies, waits for them, and re-layouts  4.52 us

profile of v2, /device:TPU:16, one launch (start us, length us, event | category | flops | bytes accessed | tf_op | source)
XLA Modules:
  0.0 113.4 jit_solution(4028146231090599752)
XLA Ops:
  0.6 108.2 %alternation.1 = (f32[64,256]{1,0:T(8,128)}, bf16[4096,256]{1,0:T(8,128)(2,1)}) custom-call(bf16[1024,4096]{1,0:T(8,128)(2,1)} %obs_hbm.1, s32[32,1024]{1,0:T(8,128)} %bitcast.1, bf16[4096,256]{1,0:T(8,128)(2,1)} %basis_hbm.1, f32[64,256]{1,0:T(8,128)} %coeff_ref.1, s32[8]{0:T(128)} %lag_ref.1, f32[8,256]{1,0:T(8,128)} %arw_ref.1), custom_call_target="tpu_custom_call" | custom-call | tf_op jit(solution)/shard_map/alternation/pallas_call | solution.py:579
  108.9 1.5 %copy.10 = f32[64,256]{1,0:T(8,128)} copy(f32[64,256]{1,0:T(8,128)} %get-tuple-element.4) | data formatting | bytes 131072
  110.4 3.0 %copy.11 = bf16[4096,256]{1,0:T(8,128)(2,1)} copy(bf16[4096,256]{1,0:T(8,128)(2,1)} %get-tuple-element.5) | data formatting | bytes 4194304

commit v3 on v2

--- a/solution.py
+++ b/solution.py
@@ -26,8 +26,8 @@
     obs_hbm, maskt_hbm, basis_hbm, coeff_ref, lag_ref, arw_ref,
     newc_ref, newb_hbm,
     obs, mt, mexp, basis, ag, dacc, rs_s, rs_r, ry_s, ry_r, rz_s, rz_r, zpart,
-    xe, px, gfull, ghalo, pgb, cn, stat1, stat2, mine,
-    ct, gacc, gown, s_opp, r_opp, s_side, r_side, s_z, r_z, nb,
+    xe, px, gfull, ghalo, rbuf, sums, pgb, cn, stat1, stat2, mine,
+    ct, gacc, gown, s_opp, r_opp, s_side, r_side, s_near, r_near, s_far, r_far, nb,
     ld_sem, ag_zs, ag_zr, ag_ys, ag_yr, ag_cs, ag_cr,
     halo_s, halo_r, gh_s, gh_r, rc_ss, rc_rs, ry_ss, ry_rs, rz_ss, rz_rs,
     st_s, st_r, opp_s, opp_rs, side_s, side_rs, z_s, z_rs,
@@ -131,8 +131,7 @@
                     ).astype(BF)
 
     load_mask().wait()
-    expand(0)
-    expand(1)
+    pl.loop(0, 2)(expand)
     pl.semaphore_wait(
         barrier,
         11 + has_prev.astype(jnp.int32) + has_next.astype(jnp.int32)
@@ -201,8 +200,7 @@
     for d in range(1, 4):
         ag_y(0, d).start()
     ag_c(0, 0).start()
-    expand(2)
-    expand(3)
+    pl.loop(2, 4)(expand)
     ends(halo, has_prev, has_next, "recv")
     px[...] = prior(xe[...], OWN, glob * OWN)
     load_basis().wait()
@@ -283,29 +281,76 @@
     for k in range(4):
         ag_c(1, k).wait_recv()
     ends(ghalo_copy, f > 0, f < 15, "start")
-    for yy in range(4):
-        for cc in range(2):
-            for zz in range(2):
-                at = 32 + yy * 256 + zz * 128 + cc * 64
-                gfull[at : at + 64] = ag[1, yy, cc, zz].astype(F32)
-
-    def fold(val):
-        return jnp.sum(val, axis=0, keepdims=True)
-
-    sums = [jnp.zeros((1, R), F32)] * 3
-    for k in (1, 2, 0, 3):
-        if k == 0:
+    def blocks(act):
+        @pl.loop(0, 4)
+        def _(yy):
+            for cc in range(2):
+                for zz in range(2):
+                    frame = pl.multiple_of(yy * 256 + zz * 128 + cc * 64, 64)
+                    place = pl.multiple_of(yy * 256 + cc * 128 + zz * 64, 64)
+                    act(yy, cc, zz, frame, place)
+
+    def widen(yy, cc, zz, frame, place):
+        gfull[pl.ds(40 + frame, OWN), :] = ag[1, yy, cc, zz].astype(F32)
+
+    blocks(widen)
+    sub8 = lax.broadcasted_iota(jnp.int32, (1, 8, R), 1)
+
+    def moved(turned, tiles):
+        n = turned.shape[0] - 4
+        a = jnp.where((tiles & 1) == 1, turned[1:], turned[:-1])
+        a = jnp.where((tiles & 2) == 2, a[2:], a[:-2])
+        return jnp.where(tiles == 4, turned[4:], a[:n]).reshape(n * 8, R)
+
+    def earlier(window, lag):
+        low = lag & 7
+        turned = pltpu.roll(window, low, 1)
+        near_rows = jnp.where(sub8 >= low, turned[1:], turned[:-1])
+        return moved(near_rows, 4 - ((sub8 * 0 + lag) >> 3))
+
+    def later(window, lag):
+        low = lag & 7
+        turned = pltpu.roll(window, (8 - low) & 7, 1)
+        near_rows = jnp.where(sub8 < 8 - low, turned[:-1], turned[1:])
+        return moved(near_rows, (sub8 * 0 + lag) >> 3)
+
+    gfull[0:8] = jnp.zeros((8, R), F32)
+    rbuf[1056:1064] = jnp.zeros((8, R), F32)
+
+    @pl.loop(0, 11)
+    def _(i):
+        @pl.when(i == 9)
+        def _():
             ends(ghalo_copy, f > 0, f < 15, "recv")
-            gfull[0:32] = ghalo[0].astype(F32)
-            gfull[1056:1088] = ghalo[1].astype(F32)
-        window = gfull[k * 256 : k * 256 + 320]
-        p = prior(window, 256, f * ROWS + k * 256)
-        pgb[k * 256 : (k + 1) * 256] = p
-        g = window[32:288]
-        sums = [sums[0] + fold(g * g), sums[1] + fold(g * p), sums[2] + fold(p * p)]
+            gfull[8:40] = ghalo[0].astype(F32)
+            gfull[1064:1096] = ghalo[1].astype(F32)
+
+        at = pl.multiple_of((i + 1) % 11 * 96, 8)
+        window = gfull[pl.ds(at, 136), :].reshape(17, 8, R)
+        r = gfull[pl.ds(40 + at, 96), :]
+        for l in range(NLAG):
+            r = r - arw_ref[l : l + 1, :] * earlier(window, lag_ref[l])
+        frame = f * ROWS + at + lax.broadcasted_iota(jnp.int32, (96, R), 0)
+        rbuf[pl.ds(at, 96), :] = jnp.where((frame >= LAGMAX) & (frame < NF), r, 0.0)
+
+    sums[...] = jnp.zeros_like(sums)
+
+    @pl.loop(0, 8)
+    def _(i):
+        at = pl.multiple_of(i * 128, 128)
+        window = rbuf[pl.ds(at, 168), :].reshape(21, 8, R)
+        p = rbuf[pl.ds(at, 128), :]
+        for l in range(NLAG):
+            p = p - arw_ref[l : l + 1, :] * later(window, lag_ref[l])
+        pgb[pl.ds(at, 128), :] = p
+        g = gfull[pl.ds(40 + at, 128), :]
+        for n, val in enumerate((g * g, g * p, p * p)):
+            sums[n] += jnp.sum(val.reshape(16, 8, R), axis=0)
 
     lane = lax.broadcasted_iota(jnp.int32, (1, 128), 1)
-    s1, s12, s2 = [jnp.sum(t, axis=1, keepdims=True) for t in sums]
+    s1, s12, s2 = [
+        jnp.sum(jnp.sum(sums[n], axis=0, keepdims=True), axis=1, keepdims=True) for n in range(3)
+    ]
     row = jnp.where(
         lane == 0, s1, jnp.where(lane == 1, s12, jnp.where(lane == 2, s2, 0.0))
     )
@@ -335,16 +380,19 @@
     ss2 = jnp.maximum(ss1 - 2.0 * b1 * s12 + b1 * b1 * s22, 0.0)
     b2 = 0.3 / jnp.sqrt(ss2 * inv + 1e-6)
     by_g, by_p = b1 + b2, b1 * b2
-    for yy in range(4):
-        for cc in range(2):
-            for zz in range(2):
-                at = yy * 256 + zz * 128 + cc * 64
-                low = ag[0, yy, cc, zz].astype(F32) - 0.0625 * (
-                    by_g * gfull[32 + at : 96 + at] - by_p * pgb[at : at + 64]
-                )
-                to = yy * 256 + cc * 128 + zz * 64
-                cn[to : to + 64] = low.astype(BF)
-        ct[:, yy * 256 : (yy + 1) * 256] = cn[yy * 256 : (yy + 1) * 256].T
+    def step(yy, cc, zz, frame, place):
+        low = ag[0, yy, cc, zz].astype(F32) - 0.0625 * (
+            by_g * gfull[pl.ds(40 + frame, OWN), :] - by_p * pgb[pl.ds(frame, OWN), :]
+        )
+        cn[pl.ds(place, OWN), :] = low.astype(BF)
+
+    blocks(step)
+
+    @pl.loop(0, 4)
+    def _(yy):
+        at = pl.multiple_of(yy * 256, 256)
+        ct[:, pl.ds(at, 256)] = cn[pl.ds(at, 256), :].T
+
     own_at = pl.multiple_of(v * OWN, OWN)
     newc_ref[...] = (
         coeff_ref[...] - by_g * zpart[mine_rows, :] + by_p * pgb[pl.ds(own_at, OWN), :]
@@ -399,29 +447,34 @@
         s_side[w, 1, 128:256] = (gacc[w, 1] + r_opp[w, 128:256].astype(F32)).astype(BF)
         side(w, 1, 1).start()
 
-    def zsum(w, d):
-        return remote(
-            s_z.at[w, d], r_z.at[w, d], z_s.at[w, d], z_rs.at[w, d], fdev((zl + d) % 4, x)
-        )
-
-    def quarter(s):
-        return (
-            pl.ds(pl.multiple_of(s // 2 * SUB, SUB), SUB),
-            pl.ds(pl.multiple_of(s % 2 * SUB, SUB), SUB),
-        )
+    near, far = fdev(zl // 2 * 2 + 1 - zl % 2, x), fdev((zl + 2) % 4, x)
+
+    def to_near(w):
+        return remote(s_near.at[w], r_near.at[w], z_s.at[w, 0], z_rs.at[w, 0], near)
+
+    def to_far(w):
+        return remote(s_far.at[w], r_far.at[w], z_s.at[w, 1], z_rs.at[w, 1], far)
+
+    def of(i):
+        return pl.ds(pl.multiple_of(i * SUB, SUB), SUB)
 
     def reduce_x(w):
         for d in range(2):
             for h in range(2):
                 side(w, d, h).wait_recv()
         gown[w] = gown[w] + r_side[w, 0].astype(F32) + r_side[w, 1].astype(F32)
-        for d in (2, 1, 3):
-            ranks, verts = quarter((zl + d) % 4)
-            s_z[w, d] = gown[w, ranks, verts].astype(BF)
-            zsum(w, d).start()
-
-    def quarter_of(w, s):
-        return nb.at[s // 2, pl.ds(pl.multiple_of(x * 1024 + w * WV + s % 2 * SUB, SUB), SUB)]
+        s_near[w] = gown[w, :, of(1 - zl % 2)].astype(BF)
+        to_near(w).start()
+
+    def reduce_near(w):
+        to_near(w).wait_recv()
+        mine_verts = of(zl % 2)
+        gown[w, :, mine_verts] = gown[w, :, mine_verts] + r_near[w].astype(F32)
+        s_far[w] = gown[w, of(1 - zl // 2), mine_verts].astype(BF)
+        to_far(w).start()
+
+    def eighth_of(w, i):
+        return pl.ds(pl.multiple_of(x * 1024 + w * WV + i * SUB, SUB), SUB)
 
     def block_of(w, xx):
         return nb.at[:, pl.ds(pl.multiple_of(xx * 1024 + w * WV, WV), WV)]
@@ -429,13 +482,13 @@
     def half_of(w, xx, t):
         return nb.at[t, pl.ds(pl.multiple_of(xx * 1024 + w * WV, WV), WV)]
 
-    def gather_z(w, d):
-        part = quarter_of(w, zl)
-        return remote(part, part, az_s.at[w, d], az_r.at[w, d], fdev((zl + d) % 4, x))
-
-    def gather_z_got(w, d):
-        part = quarter_of(w, (zl + 4 - d) % 4)
-        return remote(part, part, az_s.at[w, d], az_r.at[w, d], left)
+    def gather_far(w, got):
+        part = nb.at[1 - zl // 2 if got else zl // 2, eighth_of(w, zl % 2)]
+        return remote(part, part, az_s.at[w, 0], az_r.at[w, 0], far)
+
+    def gather_near(w, got):
+        part = nb.at[:, eighth_of(w, 1 - zl % 2 if got else zl % 2)]
+        return remote(part, part, az_s.at[w, 1], az_r.at[w, 1], near)
 
     def gather_x(w, t):
         part = block_of(w, x)
@@ -460,21 +513,21 @@
         )
 
     def update(w):
-        ranks, verts = quarter(zl)
-        acc = gown[w, ranks, verts]
-        for d in range(1, 4):
-            zsum(w, d).wait_recv()
-            acc = acc + r_z[w, d].astype(F32)
-        rows = pl.ds(pl.multiple_of(x * 1024 + w * WV + zl % 2 * SUB, SUB), SUB)
+        to_far(w).wait_recv()
+        ranks = of(zl // 2)
+        acc = gown[w, ranks, of(zl % 2)] + r_far[w].astype(F32)
+        rows = eighth_of(w, zl % 2)
         nb[zl // 2, rows, :] = (
             basis[rows, ranks].astype(F32) - (2.0 ** -6) * acc.T
         ).astype(BF)
-        for d in (2, 1, 3):
-            gather_z(w, d).start()
+        gather_far(w, False).start()
+
+    def spread_near(w):
+        gather_far(w, True).wait_recv()
+        gather_near(w, False).start()
 
     def spread(w):
-        for d in range(1, 4):
-            gather_z_got(w, d).wait_recv()
+        gather_near(w, True).wait_recv()
         gather_x(w, 0).start()
         gather_x(w, 1).start()
 
@@ -490,14 +543,16 @@
             for t in range(2):
                 store(w, xx, t).start()
 
-    for act, w in (
-        (compute, 0), (compute, 1), (join, 0), (compute, 2), (join, 1), (reduce_x, 0),
-        (compute, 3), (join, 2), (update, 0), (reduce_x, 1), (join, 3), (spread, 0),
-        (update, 1), (reduce_x, 2), (spread, 1), (reduce_x, 3), (update, 2), (pass_on, 0),
-        (update, 3), (spread, 2), (pass_on, 1), (spread, 3), (finish, 0), (pass_on, 2),
-        (finish, 1), (pass_on, 3), (finish, 2), (finish, 3),
-    ):
-        act(w)
+    @pl.loop(0, WAVES + 8)
+    def _(t):
+        for act, behind in (
+            (compute, 0), (join, 1), (spread_near, 5), (update, 4), (spread, 5),
+            (reduce_near, 3), (reduce_x, 2), (pass_on, 6), (finish, 8),
+        ):
+
+            @pl.when((t >= behind) & (t < WAVES + behind))
+            def _():
+                act(t - behind)
 
     ag_z(0).wait_send()
     for i in range(2):
@@ -519,9 +574,10 @@
                 side(w, t, h).wait_send()
             gather_x(w, t).wait_send()
             relay(w, t).wait_send()
-        for d in range(1, 4):
-            zsum(w, d).wait_send()
-            gather_z(w, d).wait_send()
+        to_near(w).wait_send()
+        to_far(w).wait_send()
+        gather_far(w, False).wait_send()
+        gather_near(w, False).wait_send()
     for w in range(WAVES):
         for xx in range(4):
             for t in range(2):
@@ -547,8 +603,10 @@
         vm((128, R), F32),
         vm((128, R), F32),
         vm((OWN, R), F32),
-        vm((ROWS + 64, R), F32),
+        vm((ROWS + 72, R), F32),
         vm((2, 32, R), BF),
+        vm((ROWS + 40, R), F32),
+        vm((3, 8, R), F32),
         vm((ROWS, R), F32),
         vm((ROWS, R), BF),
         vm((4, 1, 128), F32),
@@ -561,8 +619,10 @@
         vm((WAVES, R, WV), BF),
         vm((WAVES, 2, R, WV), BF),
         vm((WAVES, 2, R, WV), BF),
-        vm((WAVES, 4, SUB, SUB), BF),
-        vm((WAVES, 4, SUB, SUB), BF),
+        vm((WAVES, R, SUB), BF),
+        vm((WAVES, R, SUB), BF),
+        vm((WAVES, SUB, SUB), BF),
+        vm((WAVES, SUB, SUB), BF),
         vm((2, COLS, 128), BF),
         dma((3,)),
         dma((2,)), dma((2,)), dma((2, 4)), dma((2, 4)), dma((2, 4)), dma((2, 4)),
@@ -570,7 +630,7 @@
         dma((4,)), dma((4,)), dma((4,)), dma((4,)), dma, dma,
         dma((2,)), dma((2,)),
         dma((WAVES, 2)), dma((WAVES, 2)), dma((WAVES, 2, 2)), dma((WAVES, 2, 2)),
-        dma((WAVES, 4)), dma((WAVES, 4)), dma((WAVES, 4)), dma((WAVES, 4)),
+        dma((WAVES, 2)), dma((WAVES, 2)), dma((WAVES, 2)), dma((WAVES, 2)),
         dma((WAVES, 2)), dma((WAVES, 2)), dma((WAVES, 2)), dma((WAVES, 2)),
         dma((WAVES, 4, 2)),
     ]

time: 114 us -> 116 us (1.018)
  Pallas kernels: 108 us -> 110 us
    pallas_call x1, Pallas kernels: 108 us -> 110 us  [shards(): pl.pallas_call(kernel, out_shape=(jax.ShapeDtypeStruct((OWN, R), F32), ja...]
where the time goes in v3:
time: 116 us; the launch traced here: 115 us
  Pallas kernels  110 us (95%)
  local copies, waits for them, and re-layouts  4.52 us (4%)
    pallas_call x1, Pallas kernels, shards(): pl.pallas_call(kernel, out_shape=(jax.ShapeDtypeStruct((OWN, R), F32), ja...  110 us
    unnamed x2, local copies, waits for them, and re-layouts  4.52 us

profile of v3, /device:TPU:16, one launch (start us, length us, event | category | flops | bytes accessed | tf_op | source)
XLA Modules:
  0.0 115.0 jit_solution(18270348216551133665)
XLA Ops:
  0.6 109.9 %alternation.1 = (f32[64,256]{1,0:T(8,128)}, bf16[4096,256]{1,0:T(8,128)(2,1)}) custom-call(bf16[1024,4096]{1,0:T(8,128)(2,1)} %obs_hbm.1, s32[32,1024]{1,0:T(8,128)} %bitcast.1, bf16[4096,256]{1,0:T(8,128)(2,1)} %basis_hbm.1, f32[64,256]{1,0:T(8,128)} %coeff_ref.1, s32[8]{0:T(128)} %lag_ref.1, f32[8,256]{1,0:T(8,128)} %arw_ref.1), custom_call_target="tpu_custom_call" | custom-call | tf_op jit(solution)/shard_map/alternation/pallas_call | solution.py:639
  110.5 1.5 %copy.10 = f32[64,256]{1,0:T(8,128)} copy(f32[64,256]{1,0:T(8,128)} %get-tuple-element.4) | data formatting | bytes 131072
  112.0 3.0 %copy.11 = bf16[4096,256]{1,0:T(8,128)(2,1)} copy(bf16[4096,256]{1,0:T(8,128)(2,1)} %get-tuple-element.5) | data formatting | bytes 4194304

commit v4 on v3

--- a/solution.py
+++ b/solution.py
@@ -27,7 +27,7 @@
     newc_ref, newb_hbm,
     obs, mt, mexp, basis, ag, dacc, rs_s, rs_r, ry_s, ry_r, rz_s, rz_r, zpart,
     xe, px, gfull, ghalo, rbuf, sums, pgb, cn, stat1, stat2, mine,
-    ct, gacc, gown, s_opp, r_opp, s_side, r_side, s_near, r_near, s_far, r_far, nb,
+    ct, gacc, gown, s_opp, r_opp, s_side, r_side, s_z, r_z, nb,
     ld_sem, ag_zs, ag_zr, ag_ys, ag_yr, ag_cs, ag_cr,
     halo_s, halo_r, gh_s, gh_r, rc_ss, rc_rs, ry_ss, ry_rs, rz_ss, rz_rs,
     st_s, st_r, opp_s, opp_rs, side_s, side_rs, z_s, z_rs,
@@ -447,34 +447,29 @@
         s_side[w, 1, 128:256] = (gacc[w, 1] + r_opp[w, 128:256].astype(F32)).astype(BF)
         side(w, 1, 1).start()
 
-    near, far = fdev(zl // 2 * 2 + 1 - zl % 2, x), fdev((zl + 2) % 4, x)
-
-    def to_near(w):
-        return remote(s_near.at[w], r_near.at[w], z_s.at[w, 0], z_rs.at[w, 0], near)
-
-    def to_far(w):
-        return remote(s_far.at[w], r_far.at[w], z_s.at[w, 1], z_rs.at[w, 1], far)
-
-    def of(i):
-        return pl.ds(pl.multiple_of(i * SUB, SUB), SUB)
+    def zsum(w, d):
+        return remote(
+            s_z.at[w, d], r_z.at[w, d], z_s.at[w, d], z_rs.at[w, d], fdev((zl + d) % 4, x)
+        )
+
+    def quarter(s):
+        return (
+            pl.ds(pl.multiple_of(s // 2 * SUB, SUB), SUB),
+            pl.ds(pl.multiple_of(s % 2 * SUB, SUB), SUB),
+        )
 
     def reduce_x(w):
         for d in range(2):
             for h in range(2):
                 side(w, d, h).wait_recv()
         gown[w] = gown[w] + r_side[w, 0].astype(F32) + r_side[w, 1].astype(F32)
-        s_near[w] = gown[w, :, of(1 - zl % 2)].astype(BF)
-        to_near(w).start()
-
-    def reduce_near(w):
-        to_near(w).wait_recv()
-        mine_verts = of(zl % 2)
-        gown[w, :, mine_verts] = gown[w, :, mine_verts] + r_near[w].astype(F32)
-        s_far[w] = gown[w, of(1 - zl // 2), mine_verts].astype(BF)
-        to_far(w).start()
-
-    def eighth_of(w, i):
-        return pl.ds(pl.multiple_of(x * 1024 + w * WV + i * SUB, SUB), SUB)
+        for d in (2, 1, 3):
+            ranks, verts = quarter((zl + d) % 4)
+            s_z[w, d] = gown[w, ranks, verts].astype(BF)
+            zsum(w, d).start()
+
+    def quarter_of(w, s):
+        return nb.at[s // 2, pl.ds(pl.multiple_of(x * 1024 + w * WV + s % 2 * SUB, SUB), SUB)]
 
     def block_of(w, xx):
         return nb.at[:, pl.ds(pl.multiple_of(xx * 1024 + w * WV, WV), WV)]
@@ -482,13 +477,13 @@
     def half_of(w, xx, t):
         return nb.at[t, pl.ds(pl.multiple_of(xx * 1024 + w * WV, WV), WV)]
 
-    def gather_far(w, got):
-        part = nb.at[1 - zl // 2 if got else zl // 2, eighth_of(w, zl % 2)]
-        return remote(part, part, az_s.at[w, 0], az_r.at[w, 0], far)
-
-    def gather_near(w, got):
-        part = nb.at[:, eighth_of(w, 1 - zl % 2 if got else zl % 2)]
-        return remote(part, part, az_s.at[w, 1], az_r.at[w, 1], near)
+    def gather_z(w, d):
+        part = quarter_of(w, zl)
+        return remote(part, part, az_s.at[w, d], az_r.at[w, d], fdev((zl + d) % 4, x))
+
+    def gather_z_got(w, d):
+        part = quarter_of(w, (zl + 4 - d) % 4)
+        return remote(part, part, az_s.at[w, d], az_r.at[w, d], left)
 
     def gather_x(w, t):
         part = block_of(w, x)
@@ -513,21 +508,21 @@
         )
 
     def update(w):
-        to_far(w).wait_recv()
-        ranks = of(zl // 2)
-        acc = gown[w, ranks, of(zl % 2)] + r_far[w].astype(F32)
-        rows = eighth_of(w, zl % 2)
+        ranks, verts = quarter(zl)
+        acc = gown[w, ranks, verts]
+        for d in range(1, 4):
+            zsum(w, d).wait_recv()
+            acc = acc + r_z[w, d].astype(F32)
+        rows = pl.ds(pl.multiple_of(x * 1024 + w * WV + zl % 2 * SUB, SUB), SUB)
         nb[zl // 2, rows, :] = (
             basis[rows, ranks].astype(F32) - (2.0 ** -6) * acc.T
         ).astype(BF)
-        gather_far(w, False).start()
-
-    def spread_near(w):
-        gather_far(w, True).wait_recv()
-        gather_near(w, False).start()
+        for d in (2, 1, 3):
+            gather_z(w, d).start()
 
     def spread(w):
-        gather_near(w, True).wait_recv()
+        for d in range(1, 4):
+            gather_z_got(w, d).wait_recv()
         gather_x(w, 0).start()
         gather_x(w, 1).start()
 
@@ -543,16 +538,14 @@
             for t in range(2):
                 store(w, xx, t).start()
 
-    @pl.loop(0, WAVES + 8)
-    def _(t):
-        for act, behind in (
-            (compute, 0), (join, 1), (spread_near, 5), (update, 4), (spread, 5),
-            (reduce_near, 3), (reduce_x, 2), (pass_on, 6), (finish, 8),
-        ):
-
-            @pl.when((t >= behind) & (t < WAVES + behind))
-            def _():
-                act(t - behind)
+    for act, w in (
+        (compute, 0), (compute, 1), (join, 0), (compute, 2), (join, 1), (reduce_x, 0),
+        (compute, 3), (join, 2), (update, 0), (reduce_x, 1), (join, 3), (spread, 0),
+        (update, 1), (reduce_x, 2), (spread, 1), (reduce_x, 3), (update, 2), (pass_on, 0),
+        (update, 3), (spread, 2), (pass_on, 1), (spread, 3), (finish, 0), (pass_on, 2),
+        (finish, 1), (pass_on, 3), (finish, 2), (finish, 3),
+    ):
+        act(w)
 
     ag_z(0).wait_send()
     for i in range(2):
@@ -574,10 +567,9 @@
                 side(w, t, h).wait_send()
             gather_x(w, t).wait_send()
             relay(w, t).wait_send()
-        to_near(w).wait_send()
-        to_far(w).wait_send()
-        gather_far(w, False).wait_send()
-        gather_near(w, False).wait_send()
+        for d in range(1, 4):
+            zsum(w, d).wait_send()
+            gather_z(w, d).wait_send()
     for w in range(WAVES):
         for xx in range(4):
             for t in range(2):
@@ -619,10 +611,8 @@
         vm((WAVES, R, WV), BF),
         vm((WAVES, 2, R, WV), BF),
         vm((WAVES, 2, R, WV), BF),
-        vm((WAVES, R, SUB), BF),
-        vm((WAVES, R, SUB), BF),
-        vm((WAVES, SUB, SUB), BF),
-        vm((WAVES, SUB, SUB), BF),
+        vm((WAVES, 4, SUB, SUB), BF),
+        vm((WAVES, 4, SUB, SUB), BF),
         vm((2, COLS, 128), BF),
         dma((3,)),
         dma((2,)), dma((2,)), dma((2, 4)), dma((2, 4)), dma((2, 4)), dma((2, 4)),
@@ -630,7 +620,7 @@
         dma((4,)), dma((4,)), dma((4,)), dma((4,)), dma, dma,
         dma((2,)), dma((2,)),
         dma((WAVES, 2)), dma((WAVES, 2)), dma((WAVES, 2, 2)), dma((WAVES, 2, 2)),
-        dma((WAVES, 2)), dma((WAVES, 2)), dma((WAVES, 2)), dma((WAVES, 2)),
+        dma((WAVES, 4)), dma((WAVES, 4)), dma((WAVES, 4)), dma((WAVES, 4)),
         dma((WAVES, 2)), dma((WAVES, 2)), dma((WAVES, 2)), dma((WAVES, 2)),
         dma((WAVES, 4, 2)),
     ]

time: 116 us -> 114 us (0.983)
    pallas_call x1, Pallas kernels: 110 us -> 109 us  [shards(): pl.pallas_call(kernel, out_shape=(jax.ShapeDtypeStruct((OWN, R), F32), ja...]
where the time goes in v4:
time: 114 us
  Pallas kernels  109 us (96%)
  local copies, waits for them, and re-layouts  4.52 us (4%)
    pallas_call x1, Pallas kernels, shards(): pl.pallas_call(kernel, out_shape=(jax.ShapeDtypeStruct((OWN, R), F32), ja...  109 us
    unnamed x2, local copies, waits for them, and re-layouts  4.52 us

profile of v4, /device:TPU:16, one launch (start us, length us, event | category | flops | bytes accessed | tf_op | source)
XLA Modules:
  0.0 113.8 jit_solution(11323763592821132719)
XLA Ops:
  0.6 108.7 %alternation.1 = (f32[64,256]{1,0:T(8,128)}, bf16[4096,256]{1,0:T(8,128)(2,1)}) custom-call(bf16[1024,4096]{1,0:T(8,128)(2,1)} %obs_hbm.1, s32[32,1024]{1,0:T(8,128)} %bitcast.1, bf16[4096,256]{1,0:T(8,128)(2,1)} %basis_hbm.1, f32[64,256]{1,0:T(8,128)} %coeff_ref.1, s32[8]{0:T(128)} %lag_ref.1, f32[8,256]{1,0:T(8,128)} %arw_ref.1), custom_call_target="tpu_custom_call" | custom-call | tf_op jit(solution)/shard_map/alternation/pallas_call | solution.py:629
  109.3 1.5 %copy.10 = f32[64,256]{1,0:T(8,128)} copy(f32[64,256]{1,0:T(8,128)} %get-tuple-element.4) | data formatting | bytes 131072
  110.8 3.0 %copy.11 = bf16[4096,256]{1,0:T(8,128)(2,1)} copy(bf16[4096,256]{1,0:T(8,128)(2,1)} %get-tuple-element.5) | data formatting | bytes 4194304

commit v5 on v4

--- a/solution.py
+++ b/solution.py
@@ -130,8 +130,6 @@
                         m[cc * 64 : cc * 64 + 64, g : g + 1], (64, 128)
                     ).astype(BF)
 
-    load_mask().wait()
-    pl.loop(0, 2)(expand)
     pl.semaphore_wait(
         barrier,
         11 + has_prev.astype(jnp.int32) + has_next.astype(jnp.int32)
@@ -196,11 +194,13 @@
 
     ag_z(0).start()
     ends(halo, has_prev, has_next, "start")
+    load_mask().wait()
+    pl.loop(0, 2)(expand)
     ag_z(0).wait_recv()
     for d in range(1, 4):
         ag_y(0, d).start()
     ag_c(0, 0).start()
-    pl.loop(2, 4)(expand)
+    expand(2)
     ends(halo, has_prev, has_next, "recv")
     px[...] = prior(xe[...], OWN, glob * OWN)
     load_basis().wait()
@@ -241,6 +241,7 @@
             for d in range(1, 4):
                 ag_y_got(0, d).wait_recv()
                 ag_c(0, d).start()
+            expand(3)
 
         @pl.when(k >= 2)
         def _():

time: 114 us -> 115 us (level); the launches traced: 114 us -> 113 us
  no operation moved by 1% of the time
where the time goes in v5:
time: 115 us; the launch traced here: 113 us
  Pallas kernels  108 us (94%)
  local copies, waits for them, and re-layouts  4.52 us (4%)
    pallas_call x1, Pallas kernels, shards(): pl.pallas_call(kernel, out_shape=(jax.ShapeDtypeStruct((OWN, R), F32), ja...  108 us
    unnamed x2, local copies, waits for them, and re-layouts  4.52 us

profile of v5, /device:TPU:16, one launch (start us, length us, event | category | flops | bytes accessed | tf_op | source)
XLA Modules:
  0.0 112.9 jit_solution(12606252489364096914)
XLA Ops:
  0.6 107.7 %alternation.1 = (f32[64,256]{1,0:T(8,128)}, bf16[4096,256]{1,0:T(8,128)(2,1)}) custom-call(bf16[1024,4096]{1,0:T(8,128)(2,1)} %obs_hbm.1, s32[32,1024]{1,0:T(8,128)} %bitcast.1, bf16[4096,256]{1,0:T(8,128)(2,1)} %basis_hbm.1, f32[64,256]{1,0:T(8,128)} %coeff_ref.1, s32[8]{0:T(128)} %lag_ref.1, f32[8,256]{1,0:T(8,128)} %arw_ref.1), custom_call_target="tpu_custom_call" | custom-call | tf_op jit(solution)/shard_map/alternation/pallas_call | solution.py:630
  108.3 1.5 %copy.10 = f32[64,256]{1,0:T(8,128)} copy(f32[64,256]{1,0:T(8,128)} %get-tuple-element.4) | data formatting | bytes 131072
  109.8 3.0 %copy.11 = bf16[4096,256]{1,0:T(8,128)(2,1)} copy(bf16[4096,256]{1,0:T(8,128)(2,1)} %get-tuple-element.5) | data formatting | bytes 4194304
